TPU v7x, 32 devices: a whole 2x2x4 slice. The times are simulated.
32 devices in a mesh: grp: 1, lat: 1, lon: 32 (over z, y, x, core).
Axes of the slice: x: 2, y: 2, z: 4, core: 2. Of those that a mesh axis runs over, the one named last changes fastest.
Arguments:
- state: float32 [5, 128, 32, 128], P(None, 'lon', 'lat', 'grp'), may hold values from -5 to 5
- tracers: float32 [12, 32, 128, 128], P(None, 'lat', ('grp', 'lon')), may hold values from 0.1 to 1.5
- coupling: float32 [5, 5], replicated, may hold values from -0.8 to 0.8
- rates: float32 [24], replicated, may hold values from 0.05 to 0.5
- pairs: int32 [24, 3], replicated, may hold values from 0 to 11
- heat_map: int32 [12], replicated, may hold values from 0 to 3
- heat_coef: float32 [4], replicated, may hold values from 0.5 to 2
Outputs:
- state_out: float32 [5, 128, 32, 128], P(None, 'lon', 'lat', 'grp')
- tracers_out: float32 [12, 32, 128, 128], P(None, 'lat', ('grp', 'lon'))
All inputs are finite; a program needn't handle non-finite values.
Results may differ from a plain program's by a relative error of at most 0.000052.
Values sent between devices are 32-bit elements; how exact they have to be, the bound alone decides.
A program may use at most 64 MiB of HBM per device.

v0:
```python
import jax
import jax.numpy as jnp
from jax import lax
from jax.sharding import PartitionSpec as P

HIGH = lax.Precision.HIGHEST


def extended(block, sides, width, periodic):
    for axis, dim in sides:
        count = lax.axis_size(axis)
        forward = [(i, i + 1) for i in range(count - 1)]
        if periodic:
            forward.append((count - 1, 0))
        backward = [(target, source) for source, target in forward]
        low = lax.ppermute(
            lax.slice_in_dim(block, block.shape[dim] - width, None, axis=dim), axis, forward
        )
        high = lax.ppermute(lax.slice_in_dim(block, 0, width, axis=dim), axis, backward)
        block = jnp.concatenate([low, block, high], axis=dim)
    return block


def stencil(center, plus_one, plus_two, minus_one, minus_two):
    advect = -(8.0 * (plus_one - minus_one) - (plus_two - minus_two)) * (0.3 / 12.0)
    return advect + 0.1 * (plus_one + minus_one - 2.0 * center)


def tendency(fields, coupling):
    padded_x = extended(fields, (("lat", 2),), 2, False)
    padded_y = extended(fields, (("grp", 3),), 2, True)
    along_x = stencil(
        fields, padded_x[:, :, 3:-1], padded_x[:, :, 4:], padded_x[:, :, 1:-3], padded_x[:, :, :-4]
    )
    along_y = stencil(
        fields,
        padded_y[:, :, :, 3:-1],
        padded_y[:, :, :, 4:],
        padded_y[:, :, :, 1:-3],
        padded_y[:, :, :, :-4],
    )
    mixed = jnp.einsum("fg,gzxy->fzxy", coupling, fields, precision=HIGH)
    return along_x + along_y + mixed


def clamped(field, axis):
    length = field.shape[axis]
    higher = jnp.concatenate(
        [
            lax.slice_in_dim(field, 1, length, axis=axis),
            lax.slice_in_dim(field, length - 1, length, axis=axis),
        ],
        axis,
    )
    lower = jnp.concatenate(
        [
            lax.slice_in_dim(field, 0, 1, axis=axis),
            lax.slice_in_dim(field, 0, length - 1, axis=axis),
        ],
        axis,
    )
    return (higher, lower)


def mixing_of(east_diff, north_diff):
    shear = east_diff * east_diff + north_diff * north_diff
    return 0.2 * shear / (1.0 + shear)


def column_step(species, mixing_k, vertical, rates, pairs, heat_map, heat_coef):
    speed = 0.4 * vertical / (1.0 + jnp.abs(vertical))
    rising = jnp.maximum(speed, 0.0)
    sinking = jnp.minimum(speed, 0.0)
    higher, lower = clamped(species, 2)
    advect = -rising * (species - lower) - sinking * (higher - species)
    diffuse = mixing_k * (higher - 2.0 * species + lower)
    flat = species.reshape(species.shape[0], -1)
    labels = jnp.arange(species.shape[0], dtype=jnp.int32)
    first = (pairs[:, 0:1] == labels[None, :]).astype(jnp.float32)
    second = (pairs[:, 1:2] == labels[None, :]).astype(jnp.float32)
    product = (pairs[:, 2:3] == labels[None, :]).astype(jnp.float32)
    conc_a = jnp.dot(first, flat, precision=HIGH)
    conc_b = jnp.dot(second, flat, precision=HIGH)
    reaction = rates[:, None] * conc_a * conc_b
    stoich = product - first - second
    change = jnp.dot(stoich.T, reaction, precision=HIGH)
    classes = jnp.arange(heat_coef.shape[0], dtype=jnp.int32)
    weights = jnp.dot(
        (heat_map[:, None] == classes[None, :]).astype(jnp.float32), heat_coef, precision=HIGH
    )
    heat = jnp.dot(weights, change, precision=HIGH)
    renewed = species + advect + diffuse + change.reshape(species.shape)
    return (renewed, heat.reshape(mixing_k.shape))


def on_device(state, tracers, coupling, rates, pairs, heat_map, heat_coef):
    section_one = state + tendency(state, coupling)
    section_two = 0.75 * state + 0.25 * (section_one + tendency(section_one, coupling))
    stepped = state / 3.0 + 2.0 / 3.0 * (section_two + tendency(section_two, coupling))
    cols_x = tracers.shape[1]
    cols_y = tracers.shape[2]
    levels_all = tracers.shape[3]
    columns = cols_x * cols_y
    horizontal = stepped[0:2]
    padded = extended(horizontal, (("lon", 1),), 1, False)
    higher = padded[:, 2:]
    lower = padded[:, :-2]
    is_first = lax.axis_index("lon") == 0
    is_last = lax.axis_index("lon") == lax.axis_size("lon") - 1
    lower = lower.at[:, 0].set(jnp.where(is_first, horizontal[:, 0], lower[:, 0]))
    higher = higher.at[:, -1].set(jnp.where(is_last, horizontal[:, -1], higher[:, -1]))
    diffs = higher - lower
    local_mix = mixing_of(diffs[0], diffs[1])
    outgoing = jnp.transpose(jnp.stack([stepped[2], local_mix]), (0, 2, 3, 1))
    received = lax.all_to_all(outgoing, "lon", split_axis=2, concat_axis=3, tiled=True)
    received = received.reshape(2, columns, levels_all)
    vertical = received[0]
    mixing_k = received[1]
    species = tracers.reshape(tracers.shape[0], columns, levels_all)
    renewed, heat = column_step(species, mixing_k, vertical, rates, pairs, heat_map, heat_coef)
    tracers_out = renewed.reshape(tracers.shape)
    heat_cols = heat.reshape(cols_x, cols_y, levels_all)
    heat_back = lax.all_to_all(heat_cols, "lon", split_axis=2, concat_axis=1, tiled=True)
    heat_levels = jnp.transpose(heat_back, (2, 0, 1))
    state_out = stepped.at[3].set(stepped[3] + 0.5 * heat_levels)
    return (state_out, tracers_out)


def solution(mesh):
    in_specs = (
        P(None, "lon", "lat", "grp"),
        P(None, "lat", ("grp", "lon"), None),
        P(),
        P(),
        P(),
        P(),
        P(),
    )
    out_specs = (P(None, "lon", "lat", "grp"), P(None, "lat", ("grp", "lon"), None))
    return jax.shard_map(
        on_device, mesh=mesh, in_specs=in_specs, out_specs=out_specs, check_vma=False
    )
```

profile of v0, /device:TPU:0, one launch (start us, length us, event | category | flops | bytes accessed | tf_op | source)
XLA Modules:
  0.0 75.3 jit_solution(15892459844705370736)
XLA Ops:
  0.7 1.3 %fusion.88 = (f32[5,4,32,2]{3,2,1,0:T(8,128)S(1)}, f32[5,4,32,2]{3,2,1,0:T(8,128)S(1)}) fusion(f32[5,4,32,128]{3,2,1,0:T(8,128)} %param.13), kind=kLoop, calls=%fused_computation.148 | loop fusion | bytes 20480 | tf_op jit(solution)/shard_map/slice | solution.py:19
  2.0 0.7 collective-permute-start.2
  2.7 0.9 %fusion.87 = (f32[5,4,2,128]{3,2,1,0:T(2,128)S(1)}, f32[5,4,2,128]{3,2,1,0:T(2,128)S(1)}) fusion(f32[5,4,32,128]{3,2,1,0:T(8,128)} %param.13), kind=kLoop, calls=%fused_computation.147 | loop fusion | bytes 81920 | tf_op jit(solution)/shard_map/slice | solution.py:19
  3.6 0.7 collective-permute-start
  4.3 0.7 collective-permute-start.3
  5.0 0.6 collective-permute-start.1
  5.7 0.8 %slice_bitcast_fusion.3 = (s32[24]{0:T(128)S(1)}, s32[24]{0:T(128)S(1)}, s32[24]{0:T(128)S(1)}) fusion(s32[24,3]{0,1:T(4,128)} %param.17), kind=kLoop, calls=%fused_computation.137 | loop fusion | bytes 576 | tf_op jit(solution)/shard_map/eq | solution.py:81
  6.9 0.8 %convolution_multiply_fusion.1 = f32[24,16384]{1,0:T(8,128)S(1)} fusion(f32[12,16384]{1,0:T(8,128)S(1)} %reshape_reshape.6, f32[24]{0:T(128)S(1)} %copy-done.8, s32[24]{0:T(128)S(1)} %get-tuple-element.79), kind=kOutput, calls=%fused_computation.1 | convolution fusion | flops 57016608 | bytes 2359488 | tf_op jit(solution)/shard_map/dot_general | solution.py:82
  7.7 0.9 %convolution_multiply_fusion = f32[24,16384]{1,0:T(8,128)S(1)} fusion(f32[24,16384]{1,0:T(8,128)S(1)} %convolution_multiply_fusion.1, f32[12,16384]{1,0:T(8,128)S(1)} %reshape_reshape.6, s32[24]{0:T(128)S(1)} %get-tuple-element.78), kind=kOutput, calls=%fused_computation | convolution fusion | flops 57016608 | bytes 3932256 | tf_op jit(solution)/shard_map/dot_general | solution.py:83
  8.6 1.2 %fusion.63 = f32[12,16384]{1,0:T(8,128)S(1)} fusion(f32[24,16384]{1,0:T(8,128)S(1)} %convolution_multiply_fusion, s32[24]{0:T(128)S(1)} %get-tuple-element.78, s32[24]{0:T(128)S(1)} %get-tuple-element.79, s32[24]{0:T(128)S(1)} %get-tuple-element.77), kind=kOutput, calls=%fused_computation.112 | convolution fusion | flops 56625408 | bytes 2359584 | tf_op jit(solution)/shard_map/dot_general | solution.py:86
  10.0 0.6 fusion.89
  10.8 0.8 %reshape.174 = f32[32,1,512]{2,1,0:T(1,128)} reshape(f32[128,4,32]{2,1,0:T(4,128)S(1)} %bitcast.75) | data formatting | bytes 131072
  11.6 7.4 %all-to-all-start = ((f32[32,1,512]{2,1,0:T(1,128)}), f32[32,1,512]{2,1,0:T(1,128)}, u32[]{:S(2)}, u32[]{:S(2)}) async-start(f32[32,1,512]{2,1,0:T(1,128)} %reshape.174), calls=%async_computation | async-start | bytes 131072 | tf_op jit(solution)/shard_map/all_to_all | solution.py:123
  19.1 0.7 fusion.4
  19.9 1.0 %constant_dynamic-update-slice_fusion.2 = f32[5,4,32,130]{3,2,1,0:T(8,128)S(1)} fusion(f32[5,4,32,130]{3,2,1,0:T(8,128)S(1)} %get-tuple-element.72, f32[5,4,32,2]{3,2,1,0:T(8,128)} %collective-permute-done.2), kind=kLoop, calls=%fused_computation.123 | loop fusion | bytes 332800 | tf_op jit(solution)/shard_map/concatenate | solution.py:20
  21.0 1.6 %fusion.53 = f32[5,4,32,128]{3,2,1,0:T(8,128)S(1)} fusion(f32[5,4,32,128]{3,2,1,0:T(8,128)S(1)} %copy-done.2, f32[5,4,32,2]{3,2,1,0:T(8,128)} %collective-permute-done.3, f32[5,4,32,130]{3,2,1,0:T(8,128)S(1)} %constant_dynamic-update-slice_fusion.2, f32[5,4,2,128]{3,2,1,0:T(2,128)S(1)} %collective-permute-done.1, ...), kind=kLoop, calls=%fused_computation.88 | loop fusion | flops 2293760 | bytes 2319360 | tf_op jit(solution)/shard_map/add | solution.py:97
  22.8 0.7 collective-permute-start.4
  23.5 0.7 collective-permute-start.5
  24.1 0.7 fusion.2
  24.9 0.7 fusion.40
  25.9 0.7 collective-permute-start.8
  26.6 0.7 collective-permute-start.9
  27.2 0.7 fusion
  28.0 0.7 fusion.25
  28.7 0.7 fusion.82
  29.4 1.3 %collective-permute-start.12 = (f32[2,1,32,128]{3,2,1,0:T(8,128)}, f32[2,1,32,128]{3,2,1,0:T(8,128)}, u32[]{:S(2)}, u32[]{:S(2)}) collective-permute-start(f32[2,1,32,128]{3,2,1,0:T(8,128)} %get-tuple-element.60), channel_id=1, source_target_pairs={{1,0},{2,1},{3,2},{4,3},{5,4},{6,5},{7,6},{8,7},{9,8},{10,9},{11,1... | collective-permute-start | bytes 98312 | tf_op jit(solution)/shard_map/ppermute | solution.py:19
  30.7 3.6 %collective-permute-start.13 = (f32[2,1,32,128]{3,2,1,0:T(8,128)}, f32[2,1,32,128]{3,2,1,0:T(8,128)}, u32[]{:S(2)}, u32[]{:S(2)}) collective-permute-start(f32[2,1,32,128]{3,2,1,0:T(8,128)} %get-tuple-element.59), channel_id=1, source_target_pairs={{0,1},{1,2},{2,3},{3,4},{4,5},{5,6},{6,7},{7,8},{8,9},{9,10},{10,1... | collective-permute-start | bytes 98312 | tf_op jit(solution)/shard_map/ppermute | solution.py:16
  34.3 1.1 %fusion.79 = (f32[12,128,1]{2,1,0:T(8,128)}, f32[12,128,1]{2,1,0:T(8,128)S(1)}) fusion(f32[12,128,128]{2,1,0:T(8,128)S(1)} %bitcast.67), kind=kLoop, calls=%fused_computation.139 | loop fusion | bytes 24576 | tf_op jit(solution)/shard_map/slice | solution.py:57
  35.5 0.5 reshape.167
  36.0 1.5 %copy.160 = f32[12,128,1]{0,1,2:T(8,128)} copy(f32[12,128,1]{2,1,0:T(8,128)S(1)} %get-tuple-element.49) | data formatting | bytes 12288
  37.5 2.0 %copy.154 = f32[12,32,4,1]{3,2,1,0:T(4,128)S(1)} copy(f32[12,32,4,1]{0,2,1,3:T(4,128)} %bitcast.83) | data formatting | bytes 12288 | tf_op jit(solution)/shard_map/concatenate | solution.py:48
  39.5 0.8 %pad_maximum_fusion.12 = (f32[2,4,32,128]{3,2,1,0:T(8,128)S(1)}, f32[2,4,32,128]{3,2,1,0:T(8,128)S(1)}) fusion(f32[2,4,32,128]{3,2,1,0:T(8,128)S(1)} %slice-done, f32[2,1,32,128]{3,2,1,0:T(8,128)} %collective-permute-done.13, f32[2,1,32,128]{3,2,1,0:T(8,128)} %collective-permute-done.12), kind=kLoop, calls=%fused_computation.98 | loop fusion | flops 65536 | bytes 458752 | tf_op jit(solution)/shard_map/concatenate | solution.py:20
  40.3 0.8 %select_dynamic-update-slice_fusion = (f32[2,4,32,128]{3,2,1,0:T(8,128)S(1)}, f32[2,4,32,128]{3,2,1,0:T(8,128)S(1)}) fusion(f32[2,4,32,128]{3,2,1,0:T(8,128)S(1)} %get-tuple-element.75, f32[2,1,32,128]{3,2,1,0:T(8,128)} %collective-permute-done.13, pred[]{:T(512)S(6)} %eq.80, f32[5,4,32,128]{3,2,1,0:T(8,128)S(1)} %copy-done.5, ...), kind=kLoop, calls=%fused_computation.110 | loop fusion | flops 16384 | bytes 196610 | tf_op jit(solution)/shard_map/scatter | solution.py:110
  41.7 1.6 %reduce.6 = f32[32,512]{1,0:T(8,128)S(1)} reduce(f32[32,1,512]{2,1,0:T(1,128)} %all-to-all-done, f32[]{:T(128)} %broadcast.133), dimensions={1}, to_apply=%all_to_all.8.reduce_sub_computation | reduce | bytes 131076 | tf_op jit(solution)/shard_map/all_to_all | solution.py:123
  43.9 0.7 copy-done.6
  44.8 1.0 %reshape.176 = f32[32,1,1024]{2,1,0:T(1,128)} reshape(f32[128,2,4,32]{3,2,1,0:T(4,128)S(1)} %bitcast.72) | data formatting | bytes 262144
  45.8 7.2 %all-to-all-start.1 = ((f32[32,1,1024]{2,1,0:T(1,128)}), f32[32,1,1024]{2,1,0:T(1,128)S(1)}, u32[]{:S(2)}, u32[]{:S(2)}) async-start(f32[32,1,1024]{2,1,0:T(1,128)} %reshape.176), calls=%async_computation.1 | async-start | bytes 262144 | tf_op jit(solution)/shard_map/all_to_all | solution.py:115
  53.0 1.4 %fusion.80 = (f32[12,128,127]{2,1,0:T(8,128)}, f32[12,128,127]{2,1,0:T(8,128)}) fusion(f32[12,128,128]{2,1,0:T(8,128)S(1)} %bitcast.68), kind=kLoop, calls=%fused_computation.140 | loop fusion | bytes 3121152 | tf_op jit(solution)/shard_map/slice | solution.py:58
  54.5 6.8 %all-to-all-done.1 = f32[32,1,1024]{2,1,0:T(1,128)S(1)} async-done(((f32[32,1,1024]{2,1,0:T(1,128)}), f32[32,1,1024]{2,1,0:T(1,128)S(1)}, u32[]{:S(2)}, u32[]{:S(2)}) %all-to-all-start.1) | async-done | bytes 131104 | tf_op jit(solution)/shard_map/all_to_all | solution.py:115
  61.3 0.9 %reduce.7 = f32[32,1024]{1,0:T(8,128)S(1)} reduce(f32[32,1,1024]{2,1,0:T(1,128)S(1)} %all-to-all-done.1, f32[]{:T(128)} %broadcast.133), dimensions={1}, to_apply=%all_to_all.9.reduce_sub_computation | reduce | bytes 262148 | tf_op jit(solution)/shard_map/all_to_all | solution.py:115
  63.0 1.0 %maximum_negate_fusion = (f32[1,32,4,32,4]{3,1,4,2,0:T(8,128)}, f32[1,32,4,32,4]{3,1,4,2,0:T(8,128)}, f32[1,32,4,32,4]{3,1,4,2,0:T(8,128)}) fusion(f32[2,32,4,32,4]{3,1,4,2,0:T(8,128)S(1)} %bitcast.74), kind=kLoop, calls=%fused_computation.96 | loop fusion | flops 114688 | bytes 327680 | tf_op jit(solution)/shard_map/neg | solution.py:75
  63.9 1.9 %copy.149 = f32[1,32,4,32,4]{1,4,3,2,0:T(4,128)} copy(f32[1,32,4,32,4]{3,1,4,2,0:T(8,128)} %get-tuple-element.52) | data formatting | bytes 131072 | tf_op jit(solution)/shard_map/neg | solution.py:75
  65.8 1.1 %copy.150 = f32[32,4,128]{2,1,0:T(4,128)S(1)} copy(f32[32,4,128]{0,2,1:T(8,128)} %bitcast.78) | data formatting | bytes 131072 | tf_op jit(solution)/shard_map/neg | solution.py:75
  66.9 1.8 %copy.151 = f32[1,32,4,32,4]{1,4,3,2,0:T(4,128)} copy(f32[1,32,4,32,4]{3,1,4,2,0:T(8,128)} %get-tuple-element.53) | data formatting | bytes 131072 | tf_op jit(solution)/shard_map/min | solution.py:73
  68.7 1.1 %copy.152 = f32[32,4,128]{2,1,0:T(4,128)S(1)} copy(f32[32,4,128]{0,2,1:T(8,128)} %bitcast.79) | data formatting | bytes 131072 | tf_op jit(solution)/shard_map/min | solution.py:73
  69.8 0.8 %copy.155 = f32[1,32,4,32,4]{1,4,3,2,0:T(4,128)} copy(f32[1,32,4,32,4]{3,1,4,2,0:T(8,128)S(1)} %copy-done.7) | data formatting | bytes 131072 | tf_op jit(solution)/shard_map/slice | solution.py:118
  70.6 1.1 %copy.156 = f32[32,4,128]{2,1,0:T(4,128)S(1)} copy(f32[32,4,128]{0,2,1:T(8,128)} %bitcast.80) | data formatting | bytes 131072 | tf_op jit(solution)/shard_map/mul | solution.py:76
  71.7 3.6 %add_add_fusion = f32[12,32,4,128]{3,2,1,0:T(4,128)} fusion(f32[12,32,4,128]{3,2,1,0:T(4,128)S(1)} %reshape.167, f32[12,32,4,128]{3,2,1,0:T(4,128)S(1)} %copy-done.1, f32[12,32,4,1]{3,2,1,0:T(4,128)S(1)} %copy.154, f32[12,32,4,127]{3,2,1,0:T(4,128)} %bitcast.71, f32[12,32,4,127]{3,2,1,0:T(4,128)} %bitcast.70, f32[12,32,4,1]{3,2,1,0:T(4,128)S(1)} %bitcast.69, ...), kind=kLoop, calls=%fused_computation.5 | loop fusion | flops 2752512 | bytes 4128768 | tf_op jit(solution)/shard_map/add | solution.py:92
  (63 shorter events, 3.4 us)
Async XLA Ops:
  0.6 18.5 %copy-start = (f32[5,5]{1,0:T(8,128)S(1)}, f32[5,5]{1,0:T(8,128)}, u32[]{:S(2)}) copy-start(f32[5,5]{1,0:T(8,128)} %param.15) | copy-start | bytes 304
  0.6 5.8 %copy-start.1 = (f32[12,32,4,128]{3,2,1,0:T(4,128)S(1)}, f32[12,32,4,128]{3,2,1,0:T(4,128)}, u32[]{:S(2)}) copy-start(f32[12,32,4,128]{3,2,1,0:T(4,128)} %param.14) | copy-start | bytes 2359300
  0.7 6.2 %copy-start.8 = (f32[24]{0:T(128)S(1)}, f32[24]{0:T(128)}, u32[]{:S(2)}) copy-start(f32[24]{0:T(128)} %param.16) | copy-start | bytes 292
  2.0 17.9 %collective-permute-start.2 = (f32[5,4,32,2]{3,2,1,0:T(8,128)S(1)}, f32[5,4,32,2]{3,2,1,0:T(8,128)}, u32[]{:S(2)}, u32[]{:S(2)}) collective-permute-start(f32[5,4,32,2]{3,2,1,0:T(8,128)S(1)} %get-tuple-element.73), channel_id=1, source_target_pairs={{0,0},{1,1},{2,2},{3,3},{4,4},{5,5},{6,6},{7,7},{8,8},{9,9},{10,10... | collective-permute-start | bytes 15368 | tf_op jit(solution)/shard_map/ppermute | solution.py:19
  3.6 17.3 %collective-permute-start = (f32[5,4,2,128]{3,2,1,0:T(2,128)S(1)}, f32[5,4,2,128]{3,2,1,0:T(2,128)S(1)}, u32[]{:S(2)}, u32[]{:S(2)}) collective-permute-start(f32[5,4,2,128]{3,2,1,0:T(2,128)S(1)} %get-tuple-element.69), channel_id=1, source_target_pairs={} | collective-permute-start | bytes 61448 | tf_op jit(solution)/shard_map/ppermute | solution.py:19
  4.3 16.6 %collective-permute-start.3 = (f32[5,4,32,2]{3,2,1,0:T(8,128)S(1)}, f32[5,4,32,2]{3,2,1,0:T(8,128)}, u32[]{:S(2)}, u32[]{:S(2)}) collective-permute-start(f32[5,4,32,2]{3,2,1,0:T(8,128)S(1)} %get-tuple-element.74), channel_id=1, source_target_pairs={{0,0},{1,1},{2,2},{3,3},{4,4},{5,5},{6,6},{7,7},{8,8},{9,9},{10,10... | collective-permute-start | bytes 15368 | tf_op jit(solution)/shard_map/ppermute | solution.py:16
  5.0 15.9 %collective-permute-start.1 = (f32[5,4,2,128]{3,2,1,0:T(2,128)S(1)}, f32[5,4,2,128]{3,2,1,0:T(2,128)S(1)}, u32[]{:S(2)}, u32[]{:S(2)}) collective-permute-start(f32[5,4,2,128]{3,2,1,0:T(2,128)S(1)} %get-tuple-element.70), channel_id=1, source_target_pairs={} | collective-permute-start | bytes 61448 | tf_op jit(solution)/shard_map/ppermute | solution.py:16
  8.6 1.2 %copy-start.9 = (s32[12]{0:T(128)S(1)}, s32[12]{0:T(128)}, u32[]{:S(2)}) copy-start(s32[12]{0:T(128)} %param.18) | copy-start | bytes 148
  8.6 1.2 %copy-start.10 = (f32[4]{0:T(128)S(1)}, f32[4]{0:T(128)}, u32[]{:S(2)}) copy-start(f32[4]{0:T(128)} %param.19) | copy-start | bytes 52
  9.8 9.3 %copy-start.2 = (f32[5,4,32,128]{3,2,1,0:T(8,128)S(1)}, f32[5,4,32,128]{3,2,1,0:T(8,128)}, u32[]{:S(2)}) copy-start(f32[5,4,32,128]{3,2,1,0:T(8,128)} %param.13) | copy-start | bytes 983044
  11.6 29.5 %all-to-all-start = ((f32[32,1,512]{2,1,0:T(1,128)}), f32[32,1,512]{2,1,0:T(1,128)}, u32[]{:S(2)}, u32[]{:S(2)}) async-start(f32[32,1,512]{2,1,0:T(1,128)} %reshape.174), calls=%async_computation | async-start | bytes 131072 | tf_op jit(solution)/shard_map/all_to_all | solution.py:123
  22.8 2.1 %collective-permute-start.6 = (f32[5,4,32,2]{3,2,1,0:T(8,128)S(1)}, f32[5,4,32,2]{3,2,1,0:T(8,128)S(1)}, u32[]{:S(2)}, u32[]{:S(2)}) collective-permute-start(f32[5,4,32,2]{3,2,1,0:T(8,128)S(1)} %get-tuple-element.67), channel_id=1, source_target_pairs={{0,0},{1,1},{2,2},{3,3},{4,4},{5,5},{6,6},{7,7},{8,8},{9,9},{10,10... | collective-permute-start | bytes 15368 | tf_op jit(solution)/shard_map/ppermute | solution.py:19
  22.8 2.1 %collective-permute-start.7 = (f32[5,4,32,2]{3,2,1,0:T(8,128)S(1)}, f32[5,4,32,2]{3,2,1,0:T(8,128)S(1)}, u32[]{:S(2)}, u32[]{:S(2)}) collective-permute-start(f32[5,4,32,2]{3,2,1,0:T(8,128)S(1)} %get-tuple-element.68), channel_id=1, source_target_pairs={{0,0},{1,1},{2,2},{3,3},{4,4},{5,5},{6,6},{7,7},{8,8},{9,9},{10,10... | collective-permute-start | bytes 15368 | tf_op jit(solution)/shard_map/ppermute | solution.py:16
  22.8 2.1 %collective-permute-start.4 = (f32[5,4,2,128]{3,2,1,0:T(2,128)S(1)}, f32[5,4,2,128]{3,2,1,0:T(2,128)S(1)}, u32[]{:S(2)}, u32[]{:S(2)}) collective-permute-start(f32[5,4,2,128]{3,2,1,0:T(2,128)S(1)} %get-tuple-element.65), channel_id=1, source_target_pairs={} | collective-permute-start | bytes 61448 | tf_op jit(solution)/shard_map/ppermute | solution.py:19
  23.5 1.4 %collective-permute-start.5 = (f32[5,4,2,128]{3,2,1,0:T(2,128)S(1)}, f32[5,4,2,128]{3,2,1,0:T(2,128)S(1)}, u32[]{:S(2)}, u32[]{:S(2)}) collective-permute-start(f32[5,4,2,128]{3,2,1,0:T(2,128)S(1)} %get-tuple-element.66), channel_id=1, source_target_pairs={} | collective-permute-start | bytes 61448 | tf_op jit(solution)/shard_map/ppermute | solution.py:16
  25.8 2.1 %collective-permute-start.10 = (f32[5,4,32,2]{3,2,1,0:T(8,128)S(1)}, f32[5,4,32,2]{3,2,1,0:T(8,128)S(1)}, u32[]{:S(2)}, u32[]{:S(2)}) collective-permute-start(f32[5,4,32,2]{3,2,1,0:T(8,128)S(1)} %get-tuple-element.63), channel_id=1, source_target_pairs={{0,0},{1,1},{2,2},{3,3},{4,4},{5,5},{6,6},{7,7},{8,8},{9,9},{10,10... | collective-permute-start | bytes 15368 | tf_op jit(solution)/shard_map/ppermute | solution.py:19
  25.9 2.1 %collective-permute-start.11 = (f32[5,4,32,2]{3,2,1,0:T(8,128)S(1)}, f32[5,4,32,2]{3,2,1,0:T(8,128)S(1)}, u32[]{:S(2)}, u32[]{:S(2)}) collective-permute-start(f32[5,4,32,2]{3,2,1,0:T(8,128)S(1)} %get-tuple-element.64), channel_id=1, source_target_pairs={{0,0},{1,1},{2,2},{3,3},{4,4},{5,5},{6,6},{7,7},{8,8},{9,9},{10,10... | collective-permute-start | bytes 15368 | tf_op jit(solution)/shard_map/ppermute | solution.py:16
  25.9 2.1 %collective-permute-start.8 = (f32[5,4,2,128]{3,2,1,0:T(2,128)S(1)}, f32[5,4,2,128]{3,2,1,0:T(2,128)S(1)}, u32[]{:S(2)}, u32[]{:S(2)}) collective-permute-start(f32[5,4,2,128]{3,2,1,0:T(2,128)S(1)} %get-tuple-element.61), channel_id=1, source_target_pairs={} | collective-permute-start | bytes 61448 | tf_op jit(solution)/shard_map/ppermute | solution.py:19
  26.6 1.4 %collective-permute-start.9 = (f32[5,4,2,128]{3,2,1,0:T(2,128)S(1)}, f32[5,4,2,128]{3,2,1,0:T(2,128)S(1)}, u32[]{:S(2)}, u32[]{:S(2)}) collective-permute-start(f32[5,4,2,128]{3,2,1,0:T(2,128)S(1)} %get-tuple-element.62), channel_id=1, source_target_pairs={} | collective-permute-start | bytes 61448 | tf_op jit(solution)/shard_map/ppermute | solution.py:16
  28.7 6.7 %copy-start.4 = (f32[5,4,32,128]{3,2,1,0:T(8,128)}, f32[5,4,32,128]{3,2,1,0:T(8,128)S(1)}, u32[]{:S(2)}) copy-start(f32[5,4,32,128]{3,2,1,0:T(8,128)S(1)} %fusion.25) | copy-start | bytes 983044
  29.4 10.1 %collective-permute-start.12 = (f32[2,1,32,128]{3,2,1,0:T(8,128)}, f32[2,1,32,128]{3,2,1,0:T(8,128)}, u32[]{:S(2)}, u32[]{:S(2)}) collective-permute-start(f32[2,1,32,128]{3,2,1,0:T(8,128)} %get-tuple-element.60), channel_id=1, source_target_pairs={{1,0},{2,1},{3,2},{4,3},{5,4},{6,5},{7,6},{8,7},{9,8},{10,9},{11,1... | collective-permute-start | bytes 98312 | tf_op jit(solution)/shard_map/ppermute | solution.py:19
  30.7 8.8 %collective-permute-start.13 = (f32[2,1,32,128]{3,2,1,0:T(8,128)}, f32[2,1,32,128]{3,2,1,0:T(8,128)}, u32[]{:S(2)}, u32[]{:S(2)}) collective-permute-start(f32[2,1,32,128]{3,2,1,0:T(8,128)} %get-tuple-element.59), channel_id=1, source_target_pairs={{0,1},{1,2},{2,3},{3,4},{4,5},{5,6},{6,7},{7,8},{8,9},{9,10},{10,1... | collective-permute-start | bytes 98312 | tf_op jit(solution)/shard_map/ppermute | solution.py:16
  35.5 4.0 %slice-start = ((f32[5,4,32,128]{3,2,1,0:T(8,128)}), f32[2,4,32,128]{3,2,1,0:T(8,128)S(1)}, s32[]{:S(2)}) async-start(f32[5,4,32,128]{3,2,1,0:T(8,128)} %copy-done.4), calls=%async_computation.2 | async-start | bytes 262144 | tf_op jit(solution)/shard_map/slice | solution.py:104
  37.5 2.8 %copy-start.5 = (f32[5,4,32,128]{3,2,1,0:T(8,128)S(1)}, f32[5,4,32,128]{3,2,1,0:T(8,128)}, u32[]{:S(2)}) copy-start(f32[5,4,32,128]{3,2,1,0:T(8,128)} %copy-done.4) | copy-start | bytes 983044
  43.8 0.7 copy-start.6
  45.8 15.4 %all-to-all-start.1 = ((f32[32,1,1024]{2,1,0:T(1,128)}), f32[32,1,1024]{2,1,0:T(1,128)S(1)}, u32[]{:S(2)}, u32[]{:S(2)}) async-start(f32[32,1,1024]{2,1,0:T(1,128)} %reshape.176), calls=%async_computation.1 | async-start | bytes 262144 | tf_op jit(solution)/shard_map/all_to_all | solution.py:115
  63.9 5.8 %copy-start.7 = (f32[1,32,4,32,4]{3,1,4,2,0:T(8,128)S(1)}, f32[1,32,4,32,4]{3,1,4,2,0:T(8,128)}, u32[]{:S(2)}) copy-start(f32[1,32,4,32,4]{3,1,4,2,0:T(8,128)} %get-tuple-element.54) | copy-start | bytes 196612
  63.9 7.7 %copy-start.3 = (f32[12,128,1]{2,1,0:T(8,128)S(1)}, f32[12,128,1]{2,1,0:T(8,128)}, u32[]{:S(2)}) copy-start(f32[12,128,1]{2,1,0:T(8,128)} %get-tuple-element.48) | copy-start | bytes 18436
where the time goes:
time: 76.1 us; the launch traced here: 75.3 us
  starting transfers between devices  25 us (33%)
  local copies, waits for them, and re-layouts  24.5 us (32%)
  other arithmetic  11.8 us (16%)
  waiting for transfers between devices  6.83 us (9%)
  matrix products  5.94 us (8%)
  between operations  1.23 us (2%)
    all_to_all x1, starting transfers between devices, on_device(): lax.all_to_all(heat_cols, 'lon', split_axis=2, concat_axis=1, tiled=True)  7.43 us
    all_to_all x1, starting transfers between devices, on_device(): lax.all_to_all(outgoing, 'lon', split_axis=2, concat_axis=3, tiled=True)  7.17 us
    all_to_all x1, waiting for transfers between devices, on_device(): lax.all_to_all(outgoing, 'lon', split_axis=2, concat_axis=3, tiled=True)  6.78 us
    ppermute x7, starting transfers between devices, extended(): lax.ppermute(lax.slice_in_dim(block, block.shape[dim] - width, None, axis...  6.37 us
    unnamed x28, local copies, waits for them, and re-layouts  4.56 us
    ppermute x7, starting transfers between devices, extended(): lax.ppermute(lax.slice_in_dim(block, 0, width, axis=dim), axis, backward)  4.03 us
    add x1, other arithmetic, column_step(): renewed = species + advect + diffuse + change.reshape(species.shape)  3.6 us
    neg x2, local copies, waits for them, and re-layouts, column_step(): advect = -rising * (species - lower) - sinking * (higher - species)  2.94 us
  transfers between devices with their start and end apart: 16, of which 1 were waited for; matrix products, arithmetic and copies ran while one was open for 30% of the time, Pallas kernels for 0%

commit v1 on v0

v1 whole, which is shorter than its diff:
```python
import functools

import jax
import jax.numpy as jnp
from jax import lax
from jax.experimental import pallas as pl
from jax.experimental.pallas import tpu as pltpu
from jax.sharding import PartitionSpec as P

HIGH = lax.Precision.HIGHEST


def extended(block, sides, width, periodic):
    for axis, dim in sides:
        count = lax.axis_size(axis)
        forward = [(i, i + 1) for i in range(count - 1)]
        if periodic:
            forward.append((count - 1, 0))
        backward = [(target, source) for source, target in forward]
        low = lax.ppermute(
            lax.slice_in_dim(block, block.shape[dim] - width, None, axis=dim), axis, forward
        )
        high = lax.ppermute(lax.slice_in_dim(block, 0, width, axis=dim), axis, backward)
        block = jnp.concatenate([low, block, high], axis=dim)
    return block


def stencil(center, plus_one, plus_two, minus_one, minus_two):
    advect = -(8.0 * (plus_one - minus_one) - (plus_two - minus_two)) * (0.3 / 12.0)
    return advect + 0.1 * (plus_one + minus_one - 2.0 * center)


def tendency(fields, coupling):
    padded_x = extended(fields, (("lat", 2),), 2, False)
    padded_y = extended(fields, (("grp", 3),), 2, True)
    along_x = stencil(
        fields, padded_x[:, :, 3:-1], padded_x[:, :, 4:], padded_x[:, :, 1:-3], padded_x[:, :, :-4]
    )
    along_y = stencil(
        fields,
        padded_y[:, :, :, 3:-1],
        padded_y[:, :, :, 4:],
        padded_y[:, :, :, 1:-3],
        padded_y[:, :, :, :-4],
    )
    mixed = jnp.einsum("fg,gzxy->fzxy", coupling, fields, precision=HIGH)
    return along_x + along_y + mixed


def runge_kutta(state, coupling):
    section_one = state + tendency(state, coupling)
    section_two = 0.75 * state + 0.25 * (section_one + tendency(section_one, coupling))
    return state / 3.0 + 2.0 / 3.0 * (section_two + tendency(section_two, coupling))


def local_tendency(planes, coupling_ref, pad_ref):
    rows, lanes = planes[0].shape
    for a, plane in enumerate(planes):
        pad_ref[a, 8 : 8 + rows, :] = plane
    result = []
    for a, plane in enumerate(planes):
        plus_one = pad_ref[a, 9 : 9 + rows, :] + pltpu.roll(plane, lanes - 1, 1)
        minus_one = pad_ref[a, 7 : 7 + rows, :] + pltpu.roll(plane, 1, 1)
        plus_two = pad_ref[a, 10 : 10 + rows, :] + pltpu.roll(plane, lanes - 2, 1)
        minus_two = pad_ref[a, 6 : 6 + rows, :] + pltpu.roll(plane, 2, 1)
        total = 0.3 * minus_one - 0.1 * plus_one + 0.025 * (plus_two - minus_two) - 0.4 * plane
        for b, other in enumerate(planes):
            total = total + coupling_ref[a, b] * other
        result.append(total)
    return result


def swap_blocks(blocks):
    blocks = list(blocks)
    rows, lanes = blocks[0].shape
    lane = lax.broadcasted_iota(jnp.int32, (rows, lanes), 1)
    step = 1
    while step < len(blocks):
        upper = (lane & step) != 0
        for i in range(len(blocks)):
            if i & step == 0:
                first, second = blocks[i], blocks[i + step]
                blocks[i] = jnp.where(upper, pltpu.roll(second, step, 1), first)
                blocks[i + step] = jnp.where(upper, second, pltpu.roll(first, lanes - step, 1))
        step *= 2
    return blocks


def turned(blocks):
    return jnp.transpose(jnp.concatenate(swap_blocks(blocks), axis=0))


def column_kernel(
    axis, n, local_steps,
    state_ref, tracers_ref, coupling_ref, rates_ref, pairs_ref, map_ref, coef_ref,
    state_out, tracers_out,
    pad_ref, react_ref, heat_ref, mix_ref, speed_ref, send_ref, recv_ref,
    send_sem, recv_sem, own_sem,
):
    me = lax.axis_index(axis)
    fields, depth, rows, lanes = state_ref.shape
    species, columns, levels = tracers_ref.shape
    reactions = rates_ref.shape[0]
    half = 2 * depth

    barrier = pltpu.get_barrier_semaphore()

    def greet(k, carry):
        pl.semaphore_signal(
            barrier, inc=1, device_id={axis: lax.rem(me + k, n)},
            device_id_type=pl.DeviceIdType.MESH,
        )
        return carry

    lax.fori_loop(1, n, greet, 0)

    chunk = 16
    warmth = []
    for r in range(reactions):
        a, b, p = pairs_ref[r, 0], pairs_ref[r, 1], pairs_ref[r, 2]
        warmth.append(coef_ref[map_ref[p]] - coef_ref[map_ref[a]] - coef_ref[map_ref[b]])

    def react(i, carry):
        at = pl.ds(pl.multiple_of(i * chunk, chunk), chunk)
        heat = jnp.zeros((chunk, levels), jnp.float32)
        for r in range(reactions):
            rate = rates_ref[r] * tracers_ref[pairs_ref[r, 0], at, :] * tracers_ref[pairs_ref[r, 1], at, :]
            react_ref[r, at, :] = rate
            heat = heat + warmth[r] * rate
        heat_ref[at, :] = heat
        return carry

    lax.fori_loop(0, columns // chunk, react, 0)

    if local_steps:
        pad_ref[...] = jnp.zeros_like(pad_ref)
        for z in range(depth):
            pad = pad_ref.at[z]
            base = [state_ref[a, z] for a in range(fields)]
            slope = local_tendency(base, coupling_ref, pad)
            one = [f + t for f, t in zip(base, slope)]
            slope = local_tendency(one, coupling_ref, pad)
            two = [0.75 * f + 0.25 * (s + t) for f, s, t in zip(base, one, slope)]
            slope = local_tendency(two, coupling_ref, pad)
            for a in range(fields):
                state_out[a, z] = base[a] * (1.0 / 3.0) + (2.0 / 3.0) * (two[a] + slope[a])
    else:
        state_out[...] = state_ref[...]

    heat_blocks = [heat_ref[pl.ds(y, rows, stride=depth), :] for y in range(depth)]
    winds = [turned([state_out[a, z] for z in range(depth)]) for a in range(3)]
    parts = winds + [turned(heat_blocks)]
    sub = lax.broadcasted_iota(jnp.int32, (n // 2, half, lanes), 1)
    low_rows = sub < depth
    for g in range(2):
        first = parts[2 * g].reshape(n // 2, half, lanes)
        second = parts[2 * g + 1].reshape(n // 2, half, lanes)
        send_ref[:, 0, g] = jnp.where(low_rows, first, pltpu.roll(second, depth, 1))
        send_ref[:, 1, g] = jnp.where(low_rows, pltpu.roll(first, depth, 1), second)

    pl.semaphore_wait(barrier, n - 1)
    own = pltpu.make_async_copy(send_ref.at[me // 2, lax.rem(me, 2)], recv_ref.at[me], own_sem)
    own.start()

    def give(k, carry):
        peer = lax.rem(me + k, n)
        pltpu.make_async_remote_copy(
            src_ref=send_ref.at[peer // 2, lax.rem(peer, 2)],
            dst_ref=recv_ref.at[me],
            send_sem=send_sem,
            recv_sem=recv_sem,
            device_id={axis: peer},
            device_id_type=pl.DeviceIdType.MESH,
        ).start()
        return carry

    lax.fori_loop(1, n, give, 0)

    def change(s, carry):
        total = jnp.zeros((columns, levels), jnp.float32)
        for r in range(reactions):
            a, b, p = pairs_ref[r, 0], pairs_ref[r, 1], pairs_ref[r, 2]
            sign = (p == s).astype(jnp.int32) - (a == s).astype(jnp.int32) - (b == s).astype(jnp.int32)
            total = total + sign.astype(jnp.float32) * react_ref[r]
        tracers_out[s] = tracers_ref[s] + total
        return carry

    lax.fori_loop(0, species, change, 0)

    own.wait()
    others = recv_ref.at[pl.ds(0, n - 1)]
    pltpu.make_async_copy(others, others, recv_sem).wait()

    pair = recv_ref[:, 0]
    at = lax.broadcasted_iota(jnp.int32, pair.shape, 1) & (depth - 1)
    beyond = jnp.concatenate([pltpu.roll(pair, depth - 1, 1)[1:], pair[n - 1 :]], axis=0)
    before = jnp.concatenate([pair[:1], pltpu.roll(pair, half - depth + 1, 1)[: n - 1]], axis=0)
    higher = jnp.where(at == depth - 1, beyond, pltpu.roll(pair, half - 1, 1))
    lower = jnp.where(at == 0, before, pltpu.roll(pair, 1, 1))
    square = (higher - lower) * (higher - lower)
    shear = square + pltpu.roll(square, depth, 1)
    mixing = 0.2 * shear / (1.0 + shear)
    mixing = mixing.reshape(n // 2, 2, half, lanes)
    mixing = jnp.where(low_rows, mixing[:, 0], mixing[:, 1]).reshape(levels, columns)
    other = recv_ref[:, 1].reshape(n // 2, 2, half, lanes)
    even, odd = other[:, 0], other[:, 1]
    vertical = jnp.where(low_rows, even, pltpu.roll(odd, depth, 1)).reshape(levels, columns)
    speed = 0.4 * vertical / (1.0 + jnp.abs(vertical))
    heated = jnp.where(low_rows, pltpu.roll(even, depth, 1), odd).reshape(n * depth, lanes)
    mixing, speed, heated = jnp.transpose(mixing), jnp.transpose(speed), jnp.transpose(heated)
    for z in range(depth):
        state_out[3, z] = state_out[3, z] + 0.5 * heated[z * rows : (z + 1) * rows]
    for y in range(depth):
        spread = pl.ds(y, rows, stride=depth)
        mix_ref[spread, :] = mixing[y * rows : (y + 1) * rows]
        speed_ref[spread, :] = speed[y * rows : (y + 1) * rows]
    level = lax.broadcasted_iota(jnp.int32, (columns, levels), 1)
    up = jnp.where(level == levels - 1, 0.0, mix_ref[...] - jnp.minimum(speed_ref[...], 0.0))
    down = jnp.where(level == 0, 0.0, mix_ref[...] + jnp.maximum(speed_ref[...], 0.0))
    mix_ref[...] = up
    speed_ref[...] = down

    def move(s, carry):
        conc = tracers_ref[s]
        below = conc - pltpu.roll(conc, 1, 1)
        above = pltpu.roll(below, levels - 1, 1)
        tracers_out[s] = tracers_out[s] + (mix_ref[...] * above - speed_ref[...] * below)
        return carry

    lax.fori_loop(0, species, move, 0)
    pltpu.make_async_copy(others, others, send_sem).wait()


def on_device(mesh, state, tracers, coupling, rates, pairs, heat_map, heat_coef):
    n = mesh.shape["lon"]
    local_steps = mesh.shape["lat"] == 1 and mesh.shape["grp"] == 1
    if not local_steps:
        state = runge_kutta(state, coupling)
    fields, depth, rows, lanes = state.shape
    species, levels = tracers.shape[0], tracers.shape[3]
    columns = tracers.shape[1] * tracers.shape[2]
    flat = tracers.reshape(species, columns, levels)
    vmem = pl.BlockSpec(memory_space=pltpu.VMEM)
    smem = pl.BlockSpec(memory_space=pltpu.SMEM)
    f32 = jnp.float32
    state_out, tracers_out = pl.pallas_call(
        functools.partial(column_kernel, "lon", n, local_steps),
        out_shape=(jax.ShapeDtypeStruct(state.shape, f32), jax.ShapeDtypeStruct(flat.shape, f32)),
        in_specs=[vmem] * 2 + [smem] * 5,
        out_specs=(vmem, vmem),
        scratch_shapes=[
            pltpu.VMEM((depth, fields, rows + 16, lanes), f32),
            pltpu.VMEM((rates.shape[0], columns, levels), f32),
            pltpu.VMEM((columns, levels), f32),
            pltpu.VMEM((columns, levels), f32),
            pltpu.VMEM((columns, levels), f32),
            pltpu.VMEM((n // 2, 2, 2, 2 * depth, lanes), f32),
            pltpu.VMEM((n, 2, 2 * depth, lanes), f32),
            pltpu.SemaphoreType.DMA,
            pltpu.SemaphoreType.DMA,
            pltpu.SemaphoreType.DMA,
        ],
        compiler_params=pltpu.CompilerParams(
            collective_id=0, has_side_effects=True, vmem_limit_bytes=32 * 2**20
        ),
    )(state, flat, coupling, rates, pairs, heat_map, heat_coef)
    return state_out, tracers_out.reshape(tracers.shape)


def solution(mesh):
    in_specs = (
        P(None, "lon", "lat", "grp"),
        P(None, "lat", ("grp", "lon"), None),
        P(),
        P(),
        P(),
        P(),
        P(),
    )
    out_specs = (P(None, "lon", "lat", "grp"), P(None, "lat", ("grp", "lon"), None))
    return jax.shard_map(
        functools.partial(on_device, mesh), mesh=mesh, in_specs=in_specs, out_specs=out_specs, check_vma=False
    )
```

time: 76.1 us -> 20.8 us (0.27)
  starting transfers between devices: 25 us -> 0 us
  local copies, waits for them, and re-layouts: 24.5 us -> 4.51 us
  Pallas kernels: 0 us -> 15.4 us
  other arithmetic: 11.8 us -> 0 us
  waiting for transfers between devices: 6.83 us -> 0 us
  matrix products: 5.94 us -> 0 us
    pallas_call x0 -> x1, Pallas kernels: none -> 15.4 us  [on_device(): pl.pallas_call(functools.partial(column_kernel, 'lon', n, local_steps), o...]
    all_to_all x2 -> x0, starting transfers between devices: 14.6 us -> none  [the longest x1 7.43 us: on_device(): lax.all_to_all(heat_cols, 'lon', split_axis=2, concat_axis=1, tiled=True)]
    ppermute x14 -> x0, starting transfers between devices: 10.4 us -> none  [the longest x7 6.37 us: extended(): lax.ppermute(lax.slice_in_dim(block, block.shape[dim] - width, None, axis...]
    all_to_all x2 -> x0, waiting for transfers between devices: 6.79 us -> none  [the longest x1 6.78 us: on_device(): lax.all_to_all(outgoing, 'lon', split_axis=2, concat_axis=3, tiled=True)]
    slice x12 -> x0, local copies, waits for them, and re-layouts: 6.68 us -> none  [the longest x6 2.6 us: extended(): lax.slice_in_dim(block, 0, width, axis=dim)]
    add x4 -> x0, other arithmetic: 6.59 us -> none  [the longest x1 3.6 us: column_step(): renewed = species + advect + diffuse + change.reshape(species.shape)]
    dot_general x8 -> x0, matrix products: 5.94 us -> none  [the longest x3 2.22 us: tendency(): mixed = jnp.einsum('fg,gzxy->fzxy', coupling, fields, precision=HIGH)]
    concatenate x3 -> x0, local copies, waits for them, and re-layouts: 2.97 us -> none  [the longest x1 1.96 us: clamped(): jnp.concatenate([lax.slice_in_dim(field, 1, length, axis=axis), lax.slice...]
  transfers between devices with their start and end apart: 16 -> 0, of which waited for: 1 -> 0; matrix products, arithmetic and copies ran while one was open for 30% -> 0% of each run, Pallas kernels for 0% -> 0%
where the time goes in v1:
time: 20.8 us; the launch traced here: 20.6 us
  Pallas kernels  15.4 us (74%)
  local copies, waits for them, and re-layouts  4.51 us (22%)
  between operations  0.69 us (3%)
    pallas_call x1, Pallas kernels, on_device(): pl.pallas_call(functools.partial(column_kernel, 'lon', n, local_steps), o...  15.4 us
    unnamed x15, local copies, waits for them, and re-layouts  4.51 us

profile of v1, /device:TPU:0, one launch (start us, length us, event | category | flops | bytes accessed | tf_op | source)
XLA Modules:
  0.0 20.6 jit_solution(15580411357832023759)
XLA Ops:
  0.6 0.0 copy-start.2
  0.6 0.0 copy-start.3
  0.7 0.0 copy-start.4
  0.7 0.0 copy-start.5
  0.7 0.8 %copy.9.pairs_ref = s32[24,3]{1,0:T(8,128)S(1)} copy(s32[24,3]{0,1:T(4,128)} %param.11) | data formatting | bytes 576 | tf_op args[4]
  1.5 0.0 copy-done.2
  1.5 0.0 copy-done.3
  1.5 0.0 copy-done.4
  1.5 0.0 copy-done.5
  1.5 0.0 copy-start
  1.5 1.1 %copy-done = f32[12,32,4,128]{3,2,1,0:T(4,128)S(1)} copy-done((f32[12,32,4,128]{3,2,1,0:T(4,128)S(1)}, f32[12,32,4,128]{3,2,1,0:T(4,128)}, u32[]{:S(2)}) %copy-start) | copy-done | bytes 786456
  2.6 0.0 copy-start.1
  2.6 1.0 %copy-done.1 = f32[5,4,32,128]{3,2,1,0:T(8,128)S(1)} copy-done((f32[5,4,32,128]{3,2,1,0:T(8,128)S(1)}, f32[5,4,32,128]{3,2,1,0:T(8,128)}, u32[]{:S(2)}) %copy-start.1) | copy-done | bytes 327704
  3.6 15.4 %shard_map.86 = (f32[5,4,32,128]{3,2,1,0:T(8,128)S(1)}, f32[12,128,128]{2,1,0:T(8,128)S(1)}) custom-call(f32[5,4,32,128]{3,2,1,0:T(8,128)S(1)} %copy-done.1, f32[12,128,128]{2,1,0:T(8,128)S(1)} %bitcast.2, f32[5,5]{1,0:T(8,128)S(1)} %copy-done.2, f32[24]{0:T(128)S(1)} %copy-done.3, s32[24,3]{1,0:T(8,128)S(1)} %copy.9.pairs_ref, s32[12]{0:T(128)S(1)} %copy-done.4, ...), custom_call_target="tpu_custom_call" | custom-call | tf_op jit(solution)/shard_map/pallas_call | solution.py:246
  19.0 0.7 %copy.12 = f32[5,4,32,128]{3,2,1,0:T(8,128)} copy(f32[5,4,32,128]{3,2,1,0:T(8,128)S(1)} %get-tuple-element.8) | data formatting | bytes 655360
  19.7 0.9 %copy.13 = f32[12,32,4,128]{3,2,1,0:T(4,128)} copy(f32[12,32,4,128]{3,2,1,0:T(4,128)S(1)} %bitcast.3) | data formatting | bytes 1572864
Async XLA Ops:
  0.6 0.8 %copy-start.2 = (f32[5,5]{1,0:T(8,128)S(1)}, f32[5,5]{1,0:T(8,128)}, u32[]{:S(2)}) copy-start(f32[5,5]{1,0:T(8,128)} %coupling_ref.1) | copy-start | bytes 304
  0.6 0.8 %copy-start.3 = (f32[24]{0:T(128)S(1)}, f32[24]{0:T(128)}, u32[]{:S(2)}) copy-start(f32[24]{0:T(128)} %rates_ref.1) | copy-start | bytes 292
  0.7 0.8 %copy-start.4 = (s32[12]{0:T(128)S(1)}, s32[12]{0:T(128)}, u32[]{:S(2)}) copy-start(s32[12]{0:T(128)} %map_ref.1) | copy-start | bytes 148
  0.7 0.8 %copy-start.5 = (f32[4]{0:T(128)S(1)}, f32[4]{0:T(128)}, u32[]{:S(2)}) copy-start(f32[4]{0:T(128)} %coef_ref.1) | copy-start | bytes 52
  1.5 1.1 %copy-start = (f32[12,32,4,128]{3,2,1,0:T(4,128)S(1)}, f32[12,32,4,128]{3,2,1,0:T(4,128)}, u32[]{:S(2)}) copy-start(f32[12,32,4,128]{3,2,1,0:T(4,128)} %param.8) | copy-start | bytes 2359300
  2.6 1.0 %copy-start.1 = (f32[5,4,32,128]{3,2,1,0:T(8,128)S(1)}, f32[5,4,32,128]{3,2,1,0:T(8,128)}, u32[]{:S(2)}) copy-start(f32[5,4,32,128]{3,2,1,0:T(8,128)} %state_ref.1) | copy-start | bytes 983044

commit v2 on v1

v2 whole, which is shorter than its diff:
```python
import functools

import jax
import jax.numpy as jnp
from jax import lax
from jax.experimental import pallas as pl
from jax.experimental.pallas import tpu as pltpu
from jax.sharding import PartitionSpec as P

HIGH = lax.Precision.HIGHEST


def extended(block, sides, width, periodic):
    for axis, dim in sides:
        count = lax.axis_size(axis)
        forward = [(i, i + 1) for i in range(count - 1)]
        if periodic:
            forward.append((count - 1, 0))
        backward = [(target, source) for source, target in forward]
        low = lax.ppermute(
            lax.slice_in_dim(block, block.shape[dim] - width, None, axis=dim), axis, forward
        )
        high = lax.ppermute(lax.slice_in_dim(block, 0, width, axis=dim), axis, backward)
        block = jnp.concatenate([low, block, high], axis=dim)
    return block


def stencil(center, plus_one, plus_two, minus_one, minus_two):
    advect = -(8.0 * (plus_one - minus_one) - (plus_two - minus_two)) * (0.3 / 12.0)
    return advect + 0.1 * (plus_one + minus_one - 2.0 * center)


def tendency(fields, coupling):
    padded_x = extended(fields, (("lat", 2),), 2, False)
    padded_y = extended(fields, (("grp", 3),), 2, True)
    along_x = stencil(
        fields, padded_x[:, :, 3:-1], padded_x[:, :, 4:], padded_x[:, :, 1:-3], padded_x[:, :, :-4]
    )
    along_y = stencil(
        fields,
        padded_y[:, :, :, 3:-1],
        padded_y[:, :, :, 4:],
        padded_y[:, :, :, 1:-3],
        padded_y[:, :, :, :-4],
    )
    mixed = jnp.einsum("fg,gzxy->fzxy", coupling, fields, precision=HIGH)
    return along_x + along_y + mixed


def runge_kutta(state, coupling):
    section_one = state + tendency(state, coupling)
    section_two = 0.75 * state + 0.25 * (section_one + tendency(section_one, coupling))
    return state / 3.0 + 2.0 / 3.0 * (section_two + tendency(section_two, coupling))


def local_tendency(planes, coupling_ref, pad_ref):
    rows, lanes = planes[0].shape
    for a, plane in enumerate(planes):
        pad_ref[a, 8 : 8 + rows, :] = plane
    result = []
    for a, plane in enumerate(planes):
        plus_one = pad_ref[a, 9 : 9 + rows, :] + pltpu.roll(plane, lanes - 1, 1)
        minus_one = pad_ref[a, 7 : 7 + rows, :] + pltpu.roll(plane, 1, 1)
        plus_two = pad_ref[a, 10 : 10 + rows, :] + pltpu.roll(plane, lanes - 2, 1)
        minus_two = pad_ref[a, 6 : 6 + rows, :] + pltpu.roll(plane, 2, 1)
        total = 0.3 * minus_one - 0.1 * plus_one + 0.025 * (plus_two - minus_two) - 0.4 * plane
        for b, other in enumerate(planes):
            total = total + coupling_ref[a, b] * other
        result.append(total)
    return result


def swap_blocks(blocks):
    blocks = list(blocks)
    rows, lanes = blocks[0].shape
    lane = lax.broadcasted_iota(jnp.int32, (rows, lanes), 1)
    step = 1
    while step < len(blocks):
        upper = (lane & step) != 0
        for i in range(len(blocks)):
            if i & step == 0:
                first, second = blocks[i], blocks[i + step]
                blocks[i] = jnp.where(upper, pltpu.roll(second, step, 1), first)
                blocks[i + step] = jnp.where(upper, second, pltpu.roll(first, lanes - step, 1))
        step *= 2
    return blocks


def paired(first, second, depth):
    half = 2 * depth
    first = first.reshape(-1, half, first.shape[-1])
    second = second.reshape(-1, half, second.shape[-1])
    low_rows = lax.broadcasted_iota(jnp.int32, first.shape, 1) < depth
    even = jnp.where(low_rows, first, pltpu.roll(second, depth, 1))
    odd = jnp.where(low_rows, pltpu.roll(first, depth, 1), second)
    return even, odd


def column_kernel(
    axis, n, local_steps,
    state_hbm, tracers_hbm, coupling_ref, rates_ref, pairs_ref, map_ref, coef_ref,
    state_out, tracers_out,
    state_ref, tracers_ref, pad_ref, react_ref, heat_ref, mix_ref, speed_ref, send_ref, recv_ref,
    load_sem, send_sem, recv_sem, own_sem,
):
    me = lax.axis_index(axis)
    fields, depth, rows, lanes = state_ref.shape
    species, columns, levels = tracers_ref.shape
    reactions = rates_ref.shape[0]
    groups = depth // 2

    loads = [
        pltpu.make_async_copy(
            state_hbm.at[:, pl.ds(2 * g, 2)], state_ref.at[:, pl.ds(2 * g, 2)], load_sem.at[g]
        )
        for g in range(groups)
    ]
    loads.append(pltpu.make_async_copy(tracers_hbm, tracers_ref, load_sem.at[groups]))
    for load in loads:
        load.start()

    barrier = pltpu.get_barrier_semaphore()

    def greet(k, carry):
        pl.semaphore_signal(
            barrier, inc=1, device_id={axis: lax.rem(me + k, n)},
            device_id_type=pl.DeviceIdType.MESH,
        )
        return carry

    lax.fori_loop(1, n, greet, 0)

    def weather(g):
        loads[g].wait()
        for z in (2 * g, 2 * g + 1):
            base = [state_ref[a, z] for a in range(fields)]
            if local_steps:
                pad = pad_ref.at[z]
                slope = local_tendency(base, coupling_ref, pad)
                one = [f + t for f, t in zip(base, slope)]
                slope = local_tendency(one, coupling_ref, pad)
                two = [0.75 * f + 0.25 * (s + t) for f, s, t in zip(base, one, slope)]
                slope = local_tendency(two, coupling_ref, pad)
                base = [f * (1.0 / 3.0) + (2.0 / 3.0) * (s + t) for f, s, t in zip(base, two, slope)]
            for a in range(fields):
                state_out[a, z] = base[a]

    def pack(g, heat):
        blocks = [
            jnp.transpose(jnp.concatenate([state_out[a, z] for a in range(3)] + [heat[z]], axis=0))
            for z in (2 * g, 2 * g + 1)
        ]
        even, odd = paired(blocks[0], blocks[1], depth)
        send_ref[g, :, 0] = even
        send_ref[g, :, 1] = odd

    def give(g):
        own = pltpu.make_async_copy(
            send_ref.at[g, me // 2, lax.rem(me, 2)], recv_ref.at[g, me], own_sem.at[g]
        )
        own.start()

        def one(k, carry):
            peer = lax.rem(me + k, n)
            pltpu.make_async_remote_copy(
                src_ref=send_ref.at[g, peer // 2, lax.rem(peer, 2)],
                dst_ref=recv_ref.at[g, me],
                send_sem=send_sem.at[g],
                recv_sem=recv_sem.at[g],
                device_id={axis: peer},
                device_id_type=pl.DeviceIdType.MESH,
            ).start()
            return carry

        lax.fori_loop(1, n, one, 0)
        return own

    pad_ref[:, :, 0:8, :] = jnp.zeros((depth, fields, 8, lanes), jnp.float32)
    pad_ref[:, :, 8 + rows :, :] = jnp.zeros((depth, fields, 8, lanes), jnp.float32)
    weather(0)

    warmth = []
    for r in range(reactions):
        a, b, p = pairs_ref[0, r], pairs_ref[1, r], pairs_ref[2, r]
        warmth.append(coef_ref[map_ref[p]] - coef_ref[map_ref[a]] - coef_ref[map_ref[b]])
    loads[groups].wait()
    chunk = 32

    def react(i, carry):
        at = pl.ds(pl.multiple_of(i * chunk, chunk), chunk)
        heat = jnp.zeros((chunk, levels), jnp.float32)
        for r in range(reactions):
            rate = rates_ref[r] * tracers_ref[pairs_ref[0, r], at, :] * tracers_ref[pairs_ref[1, r], at, :]
            react_ref[r, at, :] = rate
            heat = heat + warmth[r] * rate
        heat_ref[at, :] = heat
        return carry

    lax.fori_loop(0, columns // chunk, react, 0)
    heat = swap_blocks([heat_ref[pl.ds(y, rows, stride=depth), :] for y in range(depth)])

    owns = []
    for g in range(groups):
        if g:
            weather(g)
        pack(g, heat)
        if g == 0:
            pl.semaphore_wait(barrier, n - 1)
        owns.append(give(g))

    def change(s, carry):
        total = jnp.zeros((columns, levels), jnp.float32)
        for r in range(reactions):
            a, b, p = pairs_ref[0, r], pairs_ref[1, r], pairs_ref[2, r]
            sign = (p == s).astype(jnp.int32) - (a == s).astype(jnp.int32) - (b == s).astype(jnp.int32)
            total = total + sign.astype(jnp.float32) * react_ref[r]
        tracers_out[s] = tracers_ref[s] + total
        return carry

    lax.fori_loop(0, species, change, 0)

    others = recv_ref.at[0, pl.ds(0, n - 1)]
    winds = [[], [], []]
    for g in range(groups):
        owns[g].wait()
        pltpu.make_async_copy(others, others, recv_sem.at[g]).wait()
        tiles = recv_ref[g].reshape(n // 2, 2, 2 * depth, lanes)
        for z, block in zip((2 * g, 2 * g + 1), paired(tiles[:, 0], tiles[:, 1], depth)):
            block = jnp.transpose(block.reshape(n * depth, lanes))
            for a in range(3):
                winds[a].append(block[a * rows : (a + 1) * rows])
            state_out[3, z] = state_out[3, z] + 0.5 * block[3 * rows :]

    winds = [swap_blocks(blocks) for blocks in winds]
    level = lax.broadcasted_iota(jnp.int32, (rows, levels), 1)
    bottom, top = level == 0, level == levels - 1
    for y in range(depth):
        shear = jnp.zeros((rows, levels), jnp.float32)
        for wind in (winds[0][y], winds[1][y]):
            higher = jnp.where(top, wind, pltpu.roll(wind, levels - 1, 1))
            lower = jnp.where(bottom, wind, pltpu.roll(wind, 1, 1))
            shear = shear + (higher - lower) * (higher - lower)
        mixing = 0.2 * shear / (1.0 + shear)
        speed = 0.4 * winds[2][y] / (1.0 + jnp.abs(winds[2][y]))
        spread = pl.ds(y, rows, stride=depth)
        mix_ref[spread, :] = jnp.where(top, 0.0, mixing - jnp.minimum(speed, 0.0))
        speed_ref[spread, :] = jnp.where(bottom, 0.0, mixing + jnp.maximum(speed, 0.0))

    def move(s, carry):
        conc = tracers_ref[s]
        below = conc - pltpu.roll(conc, 1, 1)
        above = pltpu.roll(below, levels - 1, 1)
        tracers_out[s] = tracers_out[s] + (mix_ref[...] * above - speed_ref[...] * below)
        return carry

    lax.fori_loop(0, species, move, 0)
    for g in range(groups):
        pltpu.make_async_copy(others, others, send_sem.at[g]).wait()


def on_device(mesh, state, tracers, coupling, rates, pairs, heat_map, heat_coef):
    n = mesh.shape["lon"]
    local_steps = mesh.shape["lat"] == 1 and mesh.shape["grp"] == 1
    if not local_steps:
        state = runge_kutta(state, coupling)
    fields, depth, rows, lanes = state.shape
    species, levels = tracers.shape[0], tracers.shape[3]
    columns = tracers.shape[1] * tracers.shape[2]
    flat = tracers.reshape(species, columns, levels)
    vmem = pl.BlockSpec(memory_space=pltpu.VMEM)
    smem = pl.BlockSpec(memory_space=pltpu.SMEM)
    f32 = jnp.float32
    state_out, tracers_out = pl.pallas_call(
        functools.partial(column_kernel, "lon", n, local_steps),
        out_shape=(jax.ShapeDtypeStruct(state.shape, f32), jax.ShapeDtypeStruct(flat.shape, f32)),
        in_specs=[pl.BlockSpec(memory_space=pltpu.HBM)] * 2 + [smem] * 5,
        out_specs=(vmem, vmem),
        scratch_shapes=[
            pltpu.VMEM(state.shape, f32),
            pltpu.VMEM(flat.shape, f32),
            pltpu.VMEM((depth, fields, rows + 16, lanes), f32),
            pltpu.VMEM((rates.shape[0], columns, levels), f32),
            pltpu.VMEM((columns, levels), f32),
            pltpu.VMEM((columns, levels), f32),
            pltpu.VMEM((columns, levels), f32),
            pltpu.VMEM((depth // 2, n // 2, 2, 2 * depth, lanes), f32),
            pltpu.VMEM((depth // 2, n, 2 * depth, lanes), f32),
            pltpu.SemaphoreType.DMA((depth // 2 + 1,)),
            pltpu.SemaphoreType.DMA((depth // 2,)),
            pltpu.SemaphoreType.DMA((depth // 2,)),
            pltpu.SemaphoreType.DMA((depth // 2,)),
        ],
        compiler_params=pltpu.CompilerParams(
            collective_id=0, has_side_effects=True, vmem_limit_bytes=58 * 2**20
        ),
    )(state, flat, coupling, rates, pairs.T, heat_map, heat_coef)
    return state_out, tracers_out.reshape(tracers.shape)


def solution(mesh):
    in_specs = (
        P(None, "lon", "lat", "grp"),
        P(None, "lat", ("grp", "lon"), None),
        P(),
        P(),
        P(),
        P(),
        P(),
    )
    out_specs = (P(None, "lon", "lat", "grp"), P(None, "lat", ("grp", "lon"), None))
    return jax.shard_map(
        functools.partial(on_device, mesh), mesh=mesh, in_specs=in_specs, out_specs=out_specs, check_vma=False
    )
```

time: 20.8 us -> 22.9 us (1.10)
  Pallas kernels: 15.4 us -> 18.2 us
  local copies, waits for them, and re-layouts: 4.51 us -> 3.79 us
    pallas_call x1, Pallas kernels: 15.4 us -> 18.2 us  [on_device(): pl.pallas_call(functools.partial(column_kernel, 'lon', n, local_steps), o...]
    unnamed x15 -> x2, local copies, waits for them, and re-layouts: 4.51 us -> 3.79 us
where the time goes in v2:
time: 22.9 us; the launch traced here: 22.7 us
  Pallas kernels  18.2 us (79%)
  local copies, waits for them, and re-layouts  3.79 us (17%)
  between operations  0.64 us (3%)
    pallas_call x1, Pallas kernels, on_device(): pl.pallas_call(functools.partial(column_kernel, 'lon', n, local_steps), o...  18.2 us
    unnamed x2, local copies, waits for them, and re-layouts  3.79 us

profile of v2, /device:TPU:0, one launch (start us, length us, event | category | flops | bytes accessed | tf_op | source)
XLA Modules:
  0.0 22.7 jit_solution(1587388219003884115)
XLA Ops:
  0.6 18.2 %shard_map.86 = (f32[5,4,32,128]{3,2,1,0:T(8,128)}, f32[12,128,128]{2,1,0:T(8,128)}) custom-call(f32[5,4,32,128]{3,2,1,0:T(8,128)} %state_hbm.1, f32[12,128,128]{2,1,0:T(8,128)} %bitcast.3, f32[5,5]{1,0:T(8,128)} %coupling_ref.1, f32[24]{0:T(128)} %rates_ref.1, s32[3,24]{1,0:T(4,128)} %bitcast.5, s32[12]{0:T(128)} %map_ref.1, f32[4]{0:T(128)} %coef_ref.1), custom_call_target="tpu_custom_call" | custom-call | tf_op jit(solution)/shard_map/pallas_call | solution.py:273
  18.9 1.7 %copy.11 = f32[5,4,32,128]{3,2,1,0:T(8,128)} copy(f32[5,4,32,128]{3,2,1,0:T(8,128)} %get-tuple-element.8) | data formatting | bytes 655360
  20.6 2.1 %copy.12 = f32[12,32,4,128]{3,2,1,0:T(4,128)} copy(f32[12,32,4,128]{3,2,1,0:T(4,128)} %bitcast.4) | data formatting | bytes 1572864

commit v3 on v2

--- a/solution.py
+++ b/solution.py
@@ -98,10 +98,10 @@
 
 def column_kernel(
     axis, n, local_steps,
-    state_hbm, tracers_hbm, coupling_ref, rates_ref, pairs_ref, map_ref, coef_ref,
-    state_out, tracers_out,
-    state_ref, tracers_ref, pad_ref, react_ref, heat_ref, mix_ref, speed_ref, send_ref, recv_ref,
-    load_sem, send_sem, recv_sem, own_sem,
+    state_ref, tracers_ref, coupling_ref, rates_ref, pairs_ref, map_ref, coef_ref,
+    state_out, tracers_out, mix_ref, speed_ref,
+    pad_ref, react_ref, heat_ref, send_ref, recv_ref,
+    send_sem, recv_sem, own_sem,
 ):
     me = lax.axis_index(axis)
     fields, depth, rows, lanes = state_ref.shape
@@ -109,16 +109,6 @@
     reactions = rates_ref.shape[0]
     groups = depth // 2
 
-    loads = [
-        pltpu.make_async_copy(
-            state_hbm.at[:, pl.ds(2 * g, 2)], state_ref.at[:, pl.ds(2 * g, 2)], load_sem.at[g]
-        )
-        for g in range(groups)
-    ]
-    loads.append(pltpu.make_async_copy(tracers_hbm, tracers_ref, load_sem.at[groups]))
-    for load in loads:
-        load.start()
-
     barrier = pltpu.get_barrier_semaphore()
 
     def greet(k, carry):
@@ -131,7 +121,6 @@
     lax.fori_loop(1, n, greet, 0)
 
     def weather(g):
-        loads[g].wait()
         for z in (2 * g, 2 * g + 1):
             base = [state_ref[a, z] for a in range(fields)]
             if local_steps:
@@ -183,7 +172,6 @@
     for r in range(reactions):
         a, b, p = pairs_ref[0, r], pairs_ref[1, r], pairs_ref[2, r]
         warmth.append(coef_ref[map_ref[p]] - coef_ref[map_ref[a]] - coef_ref[map_ref[b]])
-    loads[groups].wait()
     chunk = 32
 
     def react(i, carry):
@@ -246,16 +234,27 @@
         mix_ref[spread, :] = jnp.where(top, 0.0, mixing - jnp.minimum(speed, 0.0))
         speed_ref[spread, :] = jnp.where(bottom, 0.0, mixing + jnp.maximum(speed, 0.0))
 
-    def move(s, carry):
+    for g in range(groups):
+        pltpu.make_async_copy(others, others, send_sem.at[g]).wait()
+
+
+def finish_kernel(
+    state_ref, tracers_ref, changed_ref, mix_ref, speed_ref, state_out, tracers_out, moved_ref, sem
+):
+    species, columns, levels = tracers_ref.shape
+    state_copy = pltpu.make_async_copy(state_ref, state_out, sem.at[species])
+    state_copy.start()
+    copies = []
+    for s in range(species):
         conc = tracers_ref[s]
         below = conc - pltpu.roll(conc, 1, 1)
         above = pltpu.roll(below, levels - 1, 1)
-        tracers_out[s] = tracers_out[s] + (mix_ref[...] * above - speed_ref[...] * below)
-        return carry
-
-    lax.fori_loop(0, species, move, 0)
-    for g in range(groups):
-        pltpu.make_async_copy(others, others, send_sem.at[g]).wait()
+        moved_ref[s] = changed_ref[s] + (mix_ref[...] * above - speed_ref[...] * below)
+        copies.append(pltpu.make_async_copy(moved_ref.at[s], tracers_out.at[s], sem.at[s]))
+        copies[-1].start()
+    for copy in copies:
+        copy.wait()
+    state_copy.wait()
 
 
 def on_device(mesh, state, tracers, coupling, rates, pairs, heat_map, heat_coef):
@@ -269,31 +268,41 @@
     flat = tracers.reshape(species, columns, levels)
     vmem = pl.BlockSpec(memory_space=pltpu.VMEM)
     smem = pl.BlockSpec(memory_space=pltpu.SMEM)
+    hbm = pl.BlockSpec(memory_space=pltpu.HBM)
     f32 = jnp.float32
-    state_out, tracers_out = pl.pallas_call(
+    whole_state = jax.ShapeDtypeStruct(state.shape, f32)
+    whole_flat = jax.ShapeDtypeStruct(flat.shape, f32)
+    plane = jax.ShapeDtypeStruct((columns, levels), f32)
+    stepped, changed, mix, speed = pl.pallas_call(
         functools.partial(column_kernel, "lon", n, local_steps),
-        out_shape=(jax.ShapeDtypeStruct(state.shape, f32), jax.ShapeDtypeStruct(flat.shape, f32)),
-        in_specs=[pl.BlockSpec(memory_space=pltpu.HBM)] * 2 + [smem] * 5,
-        out_specs=(vmem, vmem),
+        out_shape=(whole_state, whole_flat, plane, plane),
+        in_specs=[vmem] * 2 + [smem] * 5,
+        out_specs=(vmem,) * 4,
         scratch_shapes=[
-            pltpu.VMEM(state.shape, f32),
-            pltpu.VMEM(flat.shape, f32),
             pltpu.VMEM((depth, fields, rows + 16, lanes), f32),
             pltpu.VMEM((rates.shape[0], columns, levels), f32),
             pltpu.VMEM((columns, levels), f32),
-            pltpu.VMEM((columns, levels), f32),
-            pltpu.VMEM((columns, levels), f32),
             pltpu.VMEM((depth // 2, n // 2, 2, 2 * depth, lanes), f32),
             pltpu.VMEM((depth // 2, n, 2 * depth, lanes), f32),
-            pltpu.SemaphoreType.DMA((depth // 2 + 1,)),
             pltpu.SemaphoreType.DMA((depth // 2,)),
             pltpu.SemaphoreType.DMA((depth // 2,)),
             pltpu.SemaphoreType.DMA((depth // 2,)),
         ],
         compiler_params=pltpu.CompilerParams(
-            collective_id=0, has_side_effects=True, vmem_limit_bytes=58 * 2**20
+            collective_id=0, has_side_effects=True, vmem_limit_bytes=32 * 2**20
         ),
     )(state, flat, coupling, rates, pairs.T, heat_map, heat_coef)
+    state_out, tracers_out = pl.pallas_call(
+        finish_kernel,
+        out_shape=(whole_state, whole_flat),
+        in_specs=[vmem] * 5,
+        out_specs=(hbm, hbm),
+        scratch_shapes=[
+            pltpu.VMEM(flat.shape, f32),
+            pltpu.SemaphoreType.DMA((species + 1,)),
+        ],
+        compiler_params=pltpu.CompilerParams(vmem_limit_bytes=32 * 2**20),
+    )(stepped, flat, changed, mix, speed)
     return state_out, tracers_out.reshape(tracers.shape)
 
 

time: 22.9 us -> 20.8 us (0.908)
  Pallas kernels: 18.2 us -> 16.4 us
  local copies, waits for them, and re-layouts: 3.79 us -> 3.47 us
    pallas_call x1, Pallas kernels: 18.2 us -> 14.7 us  [on_device(): pl.pallas_call(functools.partial(column_kernel, 'lon', n, local_steps), o...]
    pallas_call x0 -> x1, Pallas kernels: none -> 1.71 us  [on_device(): pl.pallas_call(finish_kernel, out_shape=(whole_state, whole_flat), in_spe...]
    unnamed x2 -> x16, local copies, waits for them, and re-layouts: 3.79 us -> 3.47 us
where the time goes in v3:
time: 20.8 us; the launch traced here: 20.6 us
  Pallas kernels  16.4 us (79%)
  local copies, waits for them, and re-layouts  3.47 us (17%)
  between operations  0.69 us (3%)
    pallas_call x1, Pallas kernels, on_device(): pl.pallas_call(functools.partial(column_kernel, 'lon', n, local_steps), o...  14.7 us
    unnamed x16, local copies, waits for them, and re-layouts  3.47 us
    pallas_call x1, Pallas kernels, on_device(): pl.pallas_call(finish_kernel, out_shape=(whole_state, whole_flat), in_spe...  1.71 us

profile of v3, /device:TPU:0, one launch (start us, length us, event | category | flops | bytes accessed | tf_op | source)
XLA Modules:
  0.0 20.6 jit_solution(7225669930748166743)
XLA Ops:
  0.6 0.0 copy-start.4
  0.6 0.0 copy-start.5
  0.7 0.0 copy-start.6
  0.7 0.0 copy-start.7
  0.7 0.6 %copy-done.4 = s32[24,3]{0,1:T(4,128)S(1)} copy-done((s32[24,3]{0,1:T(4,128)S(1)}, s32[24,3]{0,1:T(4,128)}, u32[]{:S(2)}) %copy-start.4) | copy-done | bytes 312
  1.3 0.0 copy-done.5
  1.3 0.0 copy-done.6
  1.3 0.0 copy-done.7
  1.3 0.0 copy-start
  1.3 1.1 %copy-done = f32[12,32,4,128]{3,2,1,0:T(4,128)S(1)} copy-done((f32[12,32,4,128]{3,2,1,0:T(4,128)S(1)}, f32[12,32,4,128]{3,2,1,0:T(4,128)}, u32[]{:S(2)}) %copy-start) | copy-done | bytes 786456
  2.5 0.0 copy-start.2
  2.5 1.0 %copy-done.2 = f32[5,4,32,128]{3,2,1,0:T(8,128)S(1)} copy-done((f32[5,4,32,128]{3,2,1,0:T(8,128)S(1)}, f32[5,4,32,128]{3,2,1,0:T(8,128)}, u32[]{:S(2)}) %copy-start.2) | copy-done | bytes 327704
  3.4 0.0 copy-start.3
  3.4 0.7 %copy-done.3 = f32[5,5]{1,0:T(8,128)S(1)} copy-done((f32[5,5]{1,0:T(8,128)S(1)}, f32[5,5]{1,0:T(8,128)}, u32[]{:S(2)}) %copy-start.3) | copy-done | bytes 124
  4.1 0.0 copy-start.1
  4.1 14.7 %shard_map.86 = (f32[5,4,32,128]{3,2,1,0:T(8,128)S(1)}, f32[12,128,128]{2,1,0:T(8,128)S(1)}, f32[128,128]{1,0:T(8,128)S(1)}, f32[128,128]{1,0:T(8,128)S(1)}) custom-call(f32[5,4,32,128]{3,2,1,0:T(8,128)S(1)} %copy-done.2, f32[12,128,128]{2,1,0:T(8,128)S(1)} %bitcast.3, f32[5,5]{1,0:T(8,128)S(1)} %copy-done.3, f32[24]{0:T(128)S(1)} %copy-done.5, ...), custom_call_target="tpu_custom_call" | custom-call | tf_op jit(solution)/shard_map/pallas_call | solution.py:276
  18.8 0.0 copy-done.1
  18.8 1.7 %shard_map.87 = (f32[5,4,32,128]{3,2,1,0:T(8,128)}, f32[12,128,128]{2,1,0:T(8,128)}) custom-call(f32[5,4,32,128]{3,2,1,0:T(8,128)S(1)} %get-tuple-element.8.state_ref, f32[12,128,128]{2,1,0:T(8,128)S(1)} %bitcast.4, f32[12,128,128]{2,1,0:T(8,128)S(1)} %get-tuple-element.9.changed_ref, f32[128,128]{1,0:T(8,128)S(1)} %get-tuple-element.10.mix_ref, ...), custom_call_target="tpu_custom_call" | custom-call | tf_op jit(solution)/shard_map/pallas_call | solution.py:295
Async XLA Ops:
  0.6 0.7 %copy-start.4 = (s32[24,3]{0,1:T(4,128)S(1)}, s32[24,3]{0,1:T(4,128)}, u32[]{:S(2)}) copy-start(s32[24,3]{0,1:T(4,128)} %param.11) | copy-start | bytes 868
  0.6 0.7 %copy-start.5 = (f32[24]{0:T(128)S(1)}, f32[24]{0:T(128)}, u32[]{:S(2)}) copy-start(f32[24]{0:T(128)} %rates_ref.1) | copy-start | bytes 292
  0.7 0.7 %copy-start.6 = (s32[12]{0:T(128)S(1)}, s32[12]{0:T(128)}, u32[]{:S(2)}) copy-start(s32[12]{0:T(128)} %map_ref.1) | copy-start | bytes 148
  0.7 0.7 %copy-start.7 = (f32[4]{0:T(128)S(1)}, f32[4]{0:T(128)}, u32[]{:S(2)}) copy-start(f32[4]{0:T(128)} %coef_ref.1) | copy-start | bytes 52
  1.3 1.1 %copy-start = (f32[12,32,4,128]{3,2,1,0:T(4,128)S(1)}, f32[12,32,4,128]{3,2,1,0:T(4,128)}, u32[]{:S(2)}) copy-start(f32[12,32,4,128]{3,2,1,0:T(4,128)} %param.8) | copy-start | bytes 2359300
  2.5 1.0 %copy-start.2 = (f32[5,4,32,128]{3,2,1,0:T(8,128)S(1)}, f32[5,4,32,128]{3,2,1,0:T(8,128)}, u32[]{:S(2)}) copy-start(f32[5,4,32,128]{3,2,1,0:T(8,128)} %state_ref.1) | copy-start | bytes 983044
  3.4 0.7 %copy-start.3 = (f32[5,5]{1,0:T(8,128)S(1)}, f32[5,5]{1,0:T(8,128)}, u32[]{:S(2)}) copy-start(f32[5,5]{1,0:T(8,128)} %coupling_ref.1) | copy-start | bytes 304
  4.1 14.7 %copy-start.1 = (f32[12,32,4,128]{3,2,1,0:T(4,128)S(1)}, f32[12,32,4,128]{3,2,1,0:T(4,128)}, u32[]{:S(2)}) copy-start(f32[12,32,4,128]{3,2,1,0:T(4,128)} %param.8) | copy-start | bytes 2359300

commit v4 on v3

--- a/solution.py
+++ b/solution.py
@@ -70,6 +70,22 @@
     return result
 
 
+def step_kernel(state_ref, coupling_ref, stepped_ref, pad_ref):
+    fields, depth, rows, lanes = state_ref.shape
+    pad_ref[:, :, 0:8, :] = jnp.zeros((depth, fields, 8, lanes), jnp.float32)
+    pad_ref[:, :, 8 + rows :, :] = jnp.zeros((depth, fields, 8, lanes), jnp.float32)
+    for z in range(depth):
+        pad = pad_ref.at[z]
+        base = [state_ref[a, z] for a in range(fields)]
+        slope = local_tendency(base, coupling_ref, pad)
+        one = [f + t for f, t in zip(base, slope)]
+        slope = local_tendency(one, coupling_ref, pad)
+        two = [0.75 * f + 0.25 * (s + t) for f, s, t in zip(base, one, slope)]
+        slope = local_tendency(two, coupling_ref, pad)
+        for a in range(fields):
+            stepped_ref[a, z] = base[a] * (1.0 / 3.0) + (2.0 / 3.0) * (two[a] + slope[a])
+
+
 def swap_blocks(blocks):
     blocks = list(blocks)
     rows, lanes = blocks[0].shape
@@ -97,14 +113,14 @@
 
 
 def column_kernel(
-    axis, n, local_steps,
-    state_ref, tracers_ref, coupling_ref, rates_ref, pairs_ref, map_ref, coef_ref,
-    state_out, tracers_out, mix_ref, speed_ref,
-    pad_ref, react_ref, heat_ref, send_ref, recv_ref,
+    axis, n,
+    stepped_ref, tracers_ref, rates_ref, pairs_ref, map_ref, coef_ref,
+    warm_ref, tracers_out, mix_ref, speed_ref,
+    react_ref, heat_ref, send_ref, recv_ref,
     send_sem, recv_sem, own_sem,
 ):
     me = lax.axis_index(axis)
-    fields, depth, rows, lanes = state_ref.shape
+    depth, rows, lanes = warm_ref.shape
     species, columns, levels = tracers_ref.shape
     reactions = rates_ref.shape[0]
     groups = depth // 2
@@ -119,54 +135,6 @@
         return carry
 
     lax.fori_loop(1, n, greet, 0)
-
-    def weather(g):
-        for z in (2 * g, 2 * g + 1):
-            base = [state_ref[a, z] for a in range(fields)]
-            if local_steps:
-                pad = pad_ref.at[z]
-                slope = local_tendency(base, coupling_ref, pad)
-                one = [f + t for f, t in zip(base, slope)]
-                slope = local_tendency(one, coupling_ref, pad)
-                two = [0.75 * f + 0.25 * (s + t) for f, s, t in zip(base, one, slope)]
-                slope = local_tendency(two, coupling_ref, pad)
-                base = [f * (1.0 / 3.0) + (2.0 / 3.0) * (s + t) for f, s, t in zip(base, two, slope)]
-            for a in range(fields):
-                state_out[a, z] = base[a]
-
-    def pack(g, heat):
-        blocks = [
-            jnp.transpose(jnp.concatenate([state_out[a, z] for a in range(3)] + [heat[z]], axis=0))
-            for z in (2 * g, 2 * g + 1)
-        ]
-        even, odd = paired(blocks[0], blocks[1], depth)
-        send_ref[g, :, 0] = even
-        send_ref[g, :, 1] = odd
-
-    def give(g):
-        own = pltpu.make_async_copy(
-            send_ref.at[g, me // 2, lax.rem(me, 2)], recv_ref.at[g, me], own_sem.at[g]
-        )
-        own.start()
-
-        def one(k, carry):
-            peer = lax.rem(me + k, n)
-            pltpu.make_async_remote_copy(
-                src_ref=send_ref.at[g, peer // 2, lax.rem(peer, 2)],
-                dst_ref=recv_ref.at[g, me],
-                send_sem=send_sem.at[g],
-                recv_sem=recv_sem.at[g],
-                device_id={axis: peer},
-                device_id_type=pl.DeviceIdType.MESH,
-            ).start()
-            return carry
-
-        lax.fori_loop(1, n, one, 0)
-        return own
-
-    pad_ref[:, :, 0:8, :] = jnp.zeros((depth, fields, 8, lanes), jnp.float32)
-    pad_ref[:, :, 8 + rows :, :] = jnp.zeros((depth, fields, 8, lanes), jnp.float32)
-    weather(0)
 
     warmth = []
     for r in range(reactions):
@@ -187,14 +155,32 @@
     lax.fori_loop(0, columns // chunk, react, 0)
     heat = swap_blocks([heat_ref[pl.ds(y, rows, stride=depth), :] for y in range(depth)])
 
-    owns = []
     for g in range(groups):
-        if g:
-            weather(g)
-        pack(g, heat)
-        if g == 0:
-            pl.semaphore_wait(barrier, n - 1)
-        owns.append(give(g))
+        blocks = [
+            jnp.transpose(jnp.concatenate([stepped_ref[a, z] for a in range(3)] + [heat[z]], axis=0))
+            for z in (2 * g, 2 * g + 1)
+        ]
+        even, odd = paired(blocks[0], blocks[1], depth)
+        send_ref[:, 0, g] = even
+        send_ref[:, 1, g] = odd
+
+    pl.semaphore_wait(barrier, n - 1)
+
+    def give(k, carry):
+        peer = lax.rem(me + k, n)
+        pltpu.make_async_remote_copy(
+            src_ref=send_ref.at[peer // 2, lax.rem(peer, 2)],
+            dst_ref=recv_ref.at[me],
+            send_sem=send_sem,
+            recv_sem=recv_sem,
+            device_id={axis: peer},
+            device_id_type=pl.DeviceIdType.MESH,
+        ).start()
+        return carry
+
+    lax.fori_loop(1, n, give, 0)
+    own = pltpu.make_async_copy(send_ref.at[me // 2, lax.rem(me, 2)], recv_ref.at[me], own_sem)
+    own.start()
 
     def change(s, carry):
         total = jnp.zeros((columns, levels), jnp.float32)
@@ -207,17 +193,17 @@
 
     lax.fori_loop(0, species, change, 0)
 
-    others = recv_ref.at[0, pl.ds(0, n - 1)]
+    own.wait()
+    others = recv_ref.at[pl.ds(0, n - 1)]
+    pltpu.make_async_copy(others, others, recv_sem).wait()
     winds = [[], [], []]
     for g in range(groups):
-        owns[g].wait()
-        pltpu.make_async_copy(others, others, recv_sem.at[g]).wait()
-        tiles = recv_ref[g].reshape(n // 2, 2, 2 * depth, lanes)
+        tiles = recv_ref[:, g].reshape(n // 2, 2, 2 * depth, lanes)
         for z, block in zip((2 * g, 2 * g + 1), paired(tiles[:, 0], tiles[:, 1], depth)):
             block = jnp.transpose(block.reshape(n * depth, lanes))
             for a in range(3):
                 winds[a].append(block[a * rows : (a + 1) * rows])
-            state_out[3, z] = state_out[3, z] + 0.5 * block[3 * rows :]
+            warm_ref[z] = stepped_ref[3, z] + 0.5 * block[3 * rows :]
 
     winds = [swap_blocks(blocks) for blocks in winds]
     level = lax.broadcasted_iota(jnp.int32, (rows, levels), 1)
@@ -234,17 +220,19 @@
         mix_ref[spread, :] = jnp.where(top, 0.0, mixing - jnp.minimum(speed, 0.0))
         speed_ref[spread, :] = jnp.where(bottom, 0.0, mixing + jnp.maximum(speed, 0.0))
 
-    for g in range(groups):
-        pltpu.make_async_copy(others, others, send_sem.at[g]).wait()
+    pltpu.make_async_copy(others, others, send_sem).wait()
 
 
 def finish_kernel(
-    state_ref, tracers_ref, changed_ref, mix_ref, speed_ref, state_out, tracers_out, moved_ref, sem
+    stepped_ref, warm_ref, tracers_ref, changed_ref, mix_ref, speed_ref,
+    state_out, tracers_out, moved_ref, sem,
 ):
     species, columns, levels = tracers_ref.shape
-    state_copy = pltpu.make_async_copy(state_ref, state_out, sem.at[species])
-    state_copy.start()
     copies = []
+    for a in range(stepped_ref.shape[0]):
+        source = warm_ref if a == 3 else stepped_ref.at[a]
+        copies.append(pltpu.make_async_copy(source, state_out.at[a], sem.at[species + a]))
+        copies[-1].start()
     for s in range(species):
         conc = tracers_ref[s]
         below = conc - pltpu.roll(conc, 1, 1)
@@ -254,14 +242,10 @@
         copies[-1].start()
     for copy in copies:
         copy.wait()
-    state_copy.wait()
 
 
 def on_device(mesh, state, tracers, coupling, rates, pairs, heat_map, heat_coef):
     n = mesh.shape["lon"]
-    local_steps = mesh.shape["lat"] == 1 and mesh.shape["grp"] == 1
-    if not local_steps:
-        state = runge_kutta(state, coupling)
     fields, depth, rows, lanes = state.shape
     species, levels = tracers.shape[0], tracers.shape[3]
     columns = tracers.shape[1] * tracers.shape[2]
@@ -273,36 +257,49 @@
     whole_state = jax.ShapeDtypeStruct(state.shape, f32)
     whole_flat = jax.ShapeDtypeStruct(flat.shape, f32)
     plane = jax.ShapeDtypeStruct((columns, levels), f32)
-    stepped, changed, mix, speed = pl.pallas_call(
-        functools.partial(column_kernel, "lon", n, local_steps),
-        out_shape=(whole_state, whole_flat, plane, plane),
-        in_specs=[vmem] * 2 + [smem] * 5,
+    if mesh.shape["lat"] == 1 and mesh.shape["grp"] == 1:
+        stepped = pl.pallas_call(
+            step_kernel,
+            out_shape=whole_state,
+            in_specs=[vmem, smem],
+            out_specs=vmem,
+            scratch_shapes=[pltpu.VMEM((depth, fields, rows + 16, lanes), f32)],
+            cost_estimate=pl.CostEstimate(
+                flops=9000 * state.size, bytes_accessed=8 * state.size, transcendentals=0
+            ),
+            compiler_params=pltpu.CompilerParams(vmem_limit_bytes=32 * 2**20),
+        )(state, coupling)
+    else:
+        stepped = runge_kutta(state, coupling)
+    warm, changed, mix, speed = pl.pallas_call(
+        functools.partial(column_kernel, "lon", n),
+        out_shape=(jax.ShapeDtypeStruct(state.shape[1:], f32), whole_flat, plane, plane),
+        in_specs=[vmem] * 2 + [smem] * 4,
         out_specs=(vmem,) * 4,
         scratch_shapes=[
-            pltpu.VMEM((depth, fields, rows + 16, lanes), f32),
             pltpu.VMEM((rates.shape[0], columns, levels), f32),
             pltpu.VMEM((columns, levels), f32),
-            pltpu.VMEM((depth // 2, n // 2, 2, 2 * depth, lanes), f32),
-            pltpu.VMEM((depth // 2, n, 2 * depth, lanes), f32),
-            pltpu.SemaphoreType.DMA((depth // 2,)),
-            pltpu.SemaphoreType.DMA((depth // 2,)),
-            pltpu.SemaphoreType.DMA((depth // 2,)),
+            pltpu.VMEM((n // 2, 2, depth // 2, 2 * depth, lanes), f32),
+            pltpu.VMEM((n, depth // 2, 2 * depth, lanes), f32),
+            pltpu.SemaphoreType.DMA,
+            pltpu.SemaphoreType.DMA,
+            pltpu.SemaphoreType.DMA,
         ],
         compiler_params=pltpu.CompilerParams(
             collective_id=0, has_side_effects=True, vmem_limit_bytes=32 * 2**20
         ),
-    )(state, flat, coupling, rates, pairs.T, heat_map, heat_coef)
+    )(stepped, flat, rates, pairs.T, heat_map, heat_coef)
     state_out, tracers_out = pl.pallas_call(
         finish_kernel,
         out_shape=(whole_state, whole_flat),
-        in_specs=[vmem] * 5,
+        in_specs=[vmem] * 6,
         out_specs=(hbm, hbm),
         scratch_shapes=[
             pltpu.VMEM(flat.shape, f32),
-            pltpu.SemaphoreType.DMA((species + 1,)),
+            pltpu.SemaphoreType.DMA((species + fields,)),
         ],
         compiler_params=pltpu.CompilerParams(vmem_limit_bytes=32 * 2**20),
-    )(stepped, flat, changed, mix, speed)
+    )(stepped, warm, flat, changed, mix, speed)
     return state_out, tracers_out.reshape(tracers.shape)
 
 

time: 20.8 us -> 19.2 us (0.923)
  the two profiles are of different devices: /device:TPU:0 before, /device:TPU:15 now
where the time goes in v4:
time: 19.2 us; the launch traced here: 19 us
  Pallas kernels  16.6 us (86%)
  local copies, waits for them, and re-layouts  1.67 us (9%)
  between operations  0.71 us (4%)
    pallas_call x1, Pallas kernels, on_device(): pl.pallas_call(functools.partial(column_kernel, 'lon', n), out_shape=(jax...  13.1 us
    pallas_call x1, Pallas kernels, on_device(): pl.pallas_call(step_kernel, out_shape=whole_state, in_specs=[vmem, smem],...  1.76 us
    pallas_call x1, Pallas kernels, on_device(): pl.pallas_call(finish_kernel, out_shape=(whole_state, whole_flat), in_spe...  1.74 us
    unnamed x14, local copies, waits for them, and re-layouts  1.67 us

profile of v4, /device:TPU:15, one launch (start us, length us, event | category | flops | bytes accessed | tf_op | source)
XLA Modules:
  0.0 19.0 jit_solution(6470057206704944820)
XLA Ops:
  0.6 0.0 copy-start.5
  0.6 1.0 %copy-done.5 = f32[5,4,32,128]{3,2,1,0:T(8,128)S(1)} copy-done((f32[5,4,32,128]{3,2,1,0:T(8,128)S(1)}, f32[5,4,32,128]{3,2,1,0:T(8,128)}, u32[]{:S(2)}) %copy-start.5) | copy-done | bytes 327704
  1.6 0.0 copy-start.6
  1.6 0.7 %copy-done.6 = f32[5,5]{1,0:T(8,128)S(1)} copy-done((f32[5,5]{1,0:T(8,128)S(1)}, f32[5,5]{1,0:T(8,128)}, u32[]{:S(2)}) %copy-start.6) | copy-done | bytes 124
  2.3 0.0 copy-start
  2.3 0.0 copy-start.1
  2.3 0.0 copy-start.2
  2.3 0.0 copy-start.3
  2.3 0.0 copy-start.4
  2.3 1.8 %shard_map.86.stepped_ref = f32[5,4,32,128]{3,2,1,0:T(8,128)S(1)} custom-call(f32[5,4,32,128]{3,2,1,0:T(8,128)S(1)} %copy-done.5, f32[5,5]{1,0:T(8,128)S(1)} %copy-done.6), custom_call_target="tpu_custom_call" | custom-call | flops 737280000 | bytes 655360 | tf_op jit(solution)/shard_map/pallas_call | solution.py:261
  4.1 0.0 copy-done
  4.1 0.0 copy-done.1
  4.1 0.0 copy-done.2
  4.1 0.0 copy-done.3
  4.1 0.0 copy-done.4
  4.1 13.1 %shard_map.87 = (f32[4,32,128]{2,1,0:T(8,128)S(1)}, f32[12,128,128]{2,1,0:T(8,128)S(1)}, f32[128,128]{1,0:T(8,128)S(1)}, f32[128,128]{1,0:T(8,128)S(1)}) custom-call(f32[5,4,32,128]{3,2,1,0:T(8,128)S(1)} %shard_map.86.stepped_ref, f32[12,128,128]{2,1,0:T(8,128)S(1)} %bitcast.3, f32[24]{0:T(128)S(1)} %copy-done.2, s32[3,24]{1,0:T(4,128)S(1)} %bitcast.5, ...), custom_call_target="tpu_custom_call" | custom-call | tf_op jit(solution)/shard_map/pallas_call | solution.py:274
  17.2 1.7 %shard_map.88 = (f32[5,4,32,128]{3,2,1,0:T(8,128)}, f32[12,128,128]{2,1,0:T(8,128)}) custom-call(f32[5,4,32,128]{3,2,1,0:T(8,128)S(1)} %shard_map.86.stepped_ref, f32[4,32,128]{2,1,0:T(8,128)S(1)} %get-tuple-element.8.warm_ref, f32[12,128,128]{2,1,0:T(8,128)S(1)} %bitcast.4, f32[12,128,128]{2,1,0:T(8,128)S(1)} %get-tuple-element.9.changed_ref, ...), custom_call_target="tpu_custom_call" | custom-call | tf_op jit(solution)/shard_map/pallas_call | solution.py:292
Async XLA Ops:
  0.6 1.0 %copy-start.5 = (f32[5,4,32,128]{3,2,1,0:T(8,128)S(1)}, f32[5,4,32,128]{3,2,1,0:T(8,128)}, u32[]{:S(2)}) copy-start(f32[5,4,32,128]{3,2,1,0:T(8,128)} %state_ref.1) | copy-start | bytes 983044
  1.6 0.7 %copy-start.6 = (f32[5,5]{1,0:T(8,128)S(1)}, f32[5,5]{1,0:T(8,128)}, u32[]{:S(2)}) copy-start(f32[5,5]{1,0:T(8,128)} %coupling_ref.1) | copy-start | bytes 304
  2.3 1.8 %copy-start = (f32[12,32,4,128]{3,2,1,0:T(4,128)S(1)}, f32[12,32,4,128]{3,2,1,0:T(4,128)}, u32[]{:S(2)}) copy-start(f32[12,32,4,128]{3,2,1,0:T(4,128)} %param.8) | copy-start | bytes 2359300
  2.3 1.8 %copy-start.1 = (s32[24,3]{0,1:T(4,128)S(1)}, s32[24,3]{0,1:T(4,128)}, u32[]{:S(2)}) copy-start(s32[24,3]{0,1:T(4,128)} %param.11) | copy-start | bytes 868
  2.3 1.8 %copy-start.2 = (f32[24]{0:T(128)S(1)}, f32[24]{0:T(128)}, u32[]{:S(2)}) copy-start(f32[24]{0:T(128)} %rates_ref.1) | copy-start | bytes 292
  2.3 1.8 %copy-start.3 = (s32[12]{0:T(128)S(1)}, s32[12]{0:T(128)}, u32[]{:S(2)}) copy-start(s32[12]{0:T(128)} %map_ref.1) | copy-start | bytes 148
  2.3 1.8 %copy-start.4 = (f32[4]{0:T(128)S(1)}, f32[4]{0:T(128)}, u32[]{:S(2)}) copy-start(f32[4]{0:T(128)} %coef_ref.1) | copy-start | bytes 52

commit v5 on v4

--- a/solution.py
+++ b/solution.py
@@ -166,8 +166,8 @@
 
     pl.semaphore_wait(barrier, n - 1)
 
-    def give(k, carry):
-        peer = lax.rem(me + k, n)
+    def give(j, carry):
+        peer = lax.rem(me + 1 + lax.rem(j + n // 4 - 1, n - 1), n)
         pltpu.make_async_remote_copy(
             src_ref=send_ref.at[peer // 2, lax.rem(peer, 2)],
             dst_ref=recv_ref.at[me],
@@ -178,7 +178,7 @@
         ).start()
         return carry
 
-    lax.fori_loop(1, n, give, 0)
+    lax.fori_loop(0, n - 1, give, 0)
     own = pltpu.make_async_copy(send_ref.at[me // 2, lax.rem(me, 2)], recv_ref.at[me], own_sem)
     own.start()
 

time: 19.2 us -> 20.1 us (1.047)
  the two profiles are of different devices: /device:TPU:15 before, /device:TPU:0 now
where the time goes in v5:
time: 20.1 us; the launch traced here: 19.9 us
  Pallas kernels  17.6 us (88%)
  local copies, waits for them, and re-layouts  1.67 us (8%)
  between operations  0.71 us (4%)
    pallas_call x1, Pallas kernels, on_device(): pl.pallas_call(functools.partial(column_kernel, 'lon', n), out_shape=(jax...  14.1 us
    pallas_call x1, Pallas kernels, on_device(): pl.pallas_call(step_kernel, out_shape=whole_state, in_specs=[vmem, smem],...  1.76 us
    pallas_call x1, Pallas kernels, on_device(): pl.pallas_call(finish_kernel, out_shape=(whole_state, whole_flat), in_spe...  1.74 us
    unnamed x14, local copies, waits for them, and re-layouts  1.67 us

profile of v5, /device:TPU:0, one launch (start us, length us, event | category | flops | bytes accessed | tf_op | source)
XLA Modules:
  0.0 19.9 jit_solution(5826125518494257998)
XLA Ops:
  0.6 0.0 copy-start.5
  0.6 1.0 %copy-done.5 = f32[5,4,32,128]{3,2,1,0:T(8,128)S(1)} copy-done((f32[5,4,32,128]{3,2,1,0:T(8,128)S(1)}, f32[5,4,32,128]{3,2,1,0:T(8,128)}, u32[]{:S(2)}) %copy-start.5) | copy-done | bytes 327704
  1.6 0.0 copy-start.6
  1.6 0.7 %copy-done.6 = f32[5,5]{1,0:T(8,128)S(1)} copy-done((f32[5,5]{1,0:T(8,128)S(1)}, f32[5,5]{1,0:T(8,128)}, u32[]{:S(2)}) %copy-start.6) | copy-done | bytes 124
  2.3 0.0 copy-start
  2.3 0.0 copy-start.1
  2.3 0.0 copy-start.2
  2.3 0.0 copy-start.3
  2.3 0.0 copy-start.4
  2.3 1.8 %shard_map.86.stepped_ref = f32[5,4,32,128]{3,2,1,0:T(8,128)S(1)} custom-call(f32[5,4,32,128]{3,2,1,0:T(8,128)S(1)} %copy-done.5, f32[5,5]{1,0:T(8,128)S(1)} %copy-done.6), custom_call_target="tpu_custom_call" | custom-call | flops 737280000 | bytes 655360 | tf_op jit(solution)/shard_map/pallas_call | solution.py:261
  4.1 0.0 copy-done
  4.1 0.0 copy-done.1
  4.1 0.0 copy-done.2
  4.1 0.0 copy-done.3
  4.1 0.0 copy-done.4
  4.1 14.1 %shard_map.87 = (f32[4,32,128]{2,1,0:T(8,128)S(1)}, f32[12,128,128]{2,1,0:T(8,128)S(1)}, f32[128,128]{1,0:T(8,128)S(1)}, f32[128,128]{1,0:T(8,128)S(1)}) custom-call(f32[5,4,32,128]{3,2,1,0:T(8,128)S(1)} %shard_map.86.stepped_ref, f32[12,128,128]{2,1,0:T(8,128)S(1)} %bitcast.3, f32[24]{0:T(128)S(1)} %copy-done.2, s32[3,24]{1,0:T(4,128)S(1)} %bitcast.5, ...), custom_call_target="tpu_custom_call" | custom-call | tf_op jit(solution)/shard_map/pallas_call | solution.py:274
  18.2 1.7 %shard_map.88 = (f32[5,4,32,128]{3,2,1,0:T(8,128)}, f32[12,128,128]{2,1,0:T(8,128)}) custom-call(f32[5,4,32,128]{3,2,1,0:T(8,128)S(1)} %shard_map.86.stepped_ref, f32[4,32,128]{2,1,0:T(8,128)S(1)} %get-tuple-element.8.warm_ref, f32[12,128,128]{2,1,0:T(8,128)S(1)} %bitcast.4, f32[12,128,128]{2,1,0:T(8,128)S(1)} %get-tuple-element.9.changed_ref, ...), custom_call_target="tpu_custom_call" | custom-call | tf_op jit(solution)/shard_map/pallas_call | solution.py:292
Async XLA Ops:
  0.6 1.0 %copy-start.5 = (f32[5,4,32,128]{3,2,1,0:T(8,128)S(1)}, f32[5,4,32,128]{3,2,1,0:T(8,128)}, u32[]{:S(2)}) copy-start(f32[5,4,32,128]{3,2,1,0:T(8,128)} %state_ref.1) | copy-start | bytes 983044
  1.6 0.7 %copy-start.6 = (f32[5,5]{1,0:T(8,128)S(1)}, f32[5,5]{1,0:T(8,128)}, u32[]{:S(2)}) copy-start(f32[5,5]{1,0:T(8,128)} %coupling_ref.1) | copy-start | bytes 304
  2.3 1.8 %copy-start = (f32[12,32,4,128]{3,2,1,0:T(4,128)S(1)}, f32[12,32,4,128]{3,2,1,0:T(4,128)}, u32[]{:S(2)}) copy-start(f32[12,32,4,128]{3,2,1,0:T(4,128)} %param.8) | copy-start | bytes 2359300
  2.3 1.8 %copy-start.1 = (s32[24,3]{0,1:T(4,128)S(1)}, s32[24,3]{0,1:T(4,128)}, u32[]{:S(2)}) copy-start(s32[24,3]{0,1:T(4,128)} %param.11) | copy-start | bytes 868
  2.3 1.8 %copy-start.2 = (f32[24]{0:T(128)S(1)}, f32[24]{0:T(128)}, u32[]{:S(2)}) copy-start(f32[24]{0:T(128)} %rates_ref.1) | copy-start | bytes 292
  2.3 1.8 %copy-start.3 = (s32[12]{0:T(128)S(1)}, s32[12]{0:T(128)}, u32[]{:S(2)}) copy-start(s32[12]{0:T(128)} %map_ref.1) | copy-start | bytes 148
  2.3 1.8 %copy-start.4 = (f32[4]{0:T(128)S(1)}, f32[4]{0:T(128)}, u32[]{:S(2)}) copy-start(f32[4]{0:T(128)} %coef_ref.1) | copy-start | bytes 52
